TPU v7x, 128 devices: a whole 4x4x4 slice. The times are simulated.
128 devices in a mesh: dp: 8 (over y, z_hi), tensor: 16 (over x, z_lo, core).
Axes of the slice: x: 4, y: 4, z: 4 (z_hi: 2, z_lo: 2; z = z_hi * 2 + z_lo), core: 2. Of those that a mesh axis runs over, the one named last changes fastest.
Arguments:
- layer_input: bfloat16 [3072, 4096], P(('dp', 'tensor')), may hold values from -6 to 6
- gain_vector: float32 [4096], replicated, may hold values from 0.1 to 1.9
- w_gate: bfloat16 [4096, 14784], P(None, 'tensor'), may hold values from -0.09375 to 0.09375
- w_up: bfloat16 [4096, 14784], P(None, 'tensor'), may hold values from -0.09375 to 0.09375
- w_down: bfloat16 [14784, 4096], P('tensor'), may hold values from -0.046875 to 0.046875
- grad_out: bfloat16 [3072, 4096], P(('dp', 'tensor')), may hold values from -12 to 12
Outputs:
- input_gradient: bfloat16 [3072, 4096], P(('dp', 'tensor'))
- gain_gradient: float32 [4096], replicated
- grad_w_gate: bfloat16 [4096, 14784], P('dp', 'tensor')
- grad_w_up: bfloat16 [4096, 14784], P('dp', 'tensor')
- grad_w_down: bfloat16 [14784, 4096], P('tensor', 'dp')
All inputs are finite; a program needn't handle non-finite values.
Results may differ from a plain program's by a relative error of at most 0.024.
Values may be sent and summed in bfloat16 or wider, within the bound.
A program may use at most 192 MiB of HBM per device.

v0:
```python
import jax
import jax.numpy as jnp
from jax import lax
from jax.sharding import PartitionSpec as P


def contract_rows(left, right):
    return lax.dot_general(
        left, right, (((0,), (0,)), ((), ())), preferred_element_type=jnp.float32
    )


def contract_cols(left, right):
    return lax.dot_general(
        left, right, (((1,), (1,)), ((), ())), preferred_element_type=jnp.float32
    )


def as_rounded(value):
    return value.astype(jnp.bfloat16).astype(jnp.float32)


def body(layer_input, gain_vector, w_gate, w_up, w_down, grad_out):
    input_rows = layer_input.astype(jnp.float32)
    root_mean_square = jnp.sqrt(jnp.mean(input_rows * input_rows, axis=1, keepdims=True) + 1e-06)
    unit_input = input_rows / root_mean_square
    normed_rows = (unit_input * gain_vector).astype(jnp.bfloat16)
    normed_all, upstream = (
        lax.all_gather(normed_rows, "tensor", axis=0, tiled=True),
        lax.all_gather(grad_out, "tensor", axis=0, tiled=True),
    )
    gate = jnp.dot(normed_all, w_gate, preferred_element_type=jnp.float32)
    up = jnp.dot(normed_all, w_up, preferred_element_type=jnp.float32)
    sigma = jax.nn.sigmoid(gate)
    silu = gate * sigma
    hidden = (silu * up).astype(jnp.bfloat16)
    d_hidden = contract_cols(upstream, w_down)
    d_gate = (d_hidden * up * sigma * (1.0 + gate * (1.0 - sigma))).astype(jnp.bfloat16)
    d_up = (d_hidden * silu).astype(jnp.bfloat16)
    partial_sum = contract_cols(d_gate, w_gate) + contract_cols(d_up, w_up)
    normalized_gradient = lax.psum_scatter(
        partial_sum.astype(jnp.bfloat16), "tensor", scatter_dimension=0, tiled=True
    ).astype(jnp.float32)
    scaled_rows = gain_vector * normalized_gradient
    inner_product = jnp.mean(scaled_rows * unit_input, axis=1, keepdims=True)
    input_gradient = ((scaled_rows - unit_input * inner_product) / root_mean_square).astype(
        jnp.bfloat16
    )
    gain_gradient = lax.psum(jnp.sum(normalized_gradient * unit_input, axis=0), ("dp", "tensor"))
    gate_term = as_rounded(contract_rows(normed_all, d_gate))
    up_term = as_rounded(contract_rows(normed_all, d_up))
    down_term = as_rounded(contract_rows(hidden, upstream))
    gate_sum, up_sum, down_sum = (
        lax.psum_scatter(
            gate_term.astype(jnp.bfloat16), "dp", scatter_dimension=0, tiled=True
        ).astype(jnp.float32),
        lax.psum_scatter(
            up_term.astype(jnp.bfloat16), "dp", scatter_dimension=0, tiled=True
        ).astype(jnp.float32),
        lax.psum_scatter(
            down_term.astype(jnp.bfloat16), "dp", scatter_dimension=1, tiled=True
        ).astype(jnp.float32),
    )
    return (
        input_gradient,
        gain_gradient,
        gate_sum.astype(jnp.bfloat16),
        up_sum.astype(jnp.bfloat16),
        down_sum.astype(jnp.bfloat16),
    )


def solution(mesh):
    placed = (
        P(("dp", "tensor"), None),
        P(),
        P(None, "tensor"),
        P(None, "tensor"),
        P("tensor", None),
        P(("dp", "tensor"), None),
    )
    return jax.shard_map(
        body,
        mesh=mesh,
        in_specs=placed,
        out_specs=(
            P(("dp", "tensor"), None),
            P(),
            P("dp", "tensor"),
            P("dp", "tensor"),
            P("tensor", "dp"),
        ),
        check_vma=False,
    )
```

profile of v0, /device:TPU:0, one launch (start us, length us, event | category | flops | bytes accessed | tf_op | source)
XLA Modules:
  0.0 523.3 jit_solution(14884017945511559120)
XLA Ops:
  7.2 0.0 all-gather.5.cloned.1.call-start
  7.2 1.1 fusion.6
  8.3 1.8 multiply_convert_fusion.4
  10.0 0.0 all-gather.5.cloned.1.call-update
  10.1 0.0 all-gather.3.cloned.1.call-start
  10.1 0.7 all-gather.3.cloned.1.call-update
  10.8 0.0 reduce-scatter.5.cloned.1.call-start
  10.9 37.6 %all-gather.5.cloned.1.call-done = bf16[384,4096]{1,0:T(8,128)(2,1)} async-done(((bf16[24,4096]{1,0:T(8,128)(2,1)}), bf16[384,4096]{1,0:T(8,128)(2,1)}) %all-gather.5.cloned.1.call-update) | async-done | bytes 3145744 | tf_op jit(solution)/shard_map/all_gather | solution.py:29
  48.5 0.0 copy-start.2
  48.5 8.2 %fusion.11 = f32[384,924]{0,1:T(8,128)S(1)} fusion(bf16[384,4096]{1,0:T(8,128)(2,1)} %all-gather.5.cloned.1.call-done, bf16[4096,924]{0,1:T(8,128)(2,1)} %param.8), kind=kOutput, calls=%fused_computation.25 | convolution fusion | flops 2906652672 | bytes 12134400 | tf_op jit(solution)/shard_map/dot_general | solution.py:32
  56.7 0.0 copy-done.2
  56.7 7.5 %fusion.10 = f32[384,924]{0,1:T(8,128)} fusion(bf16[384,4096]{1,0:T(8,128)(2,1)S(1)} %copy-done.2, bf16[4096,924]{0,1:T(8,128)(2,1)} %param.9), kind=kOutput, calls=%fused_computation.24 | convolution fusion | flops 2906652672 | bytes 12134400 | tf_op jit(solution)/shard_map/dot_general | solution.py:33
  64.2 22.0 %all-gather.3.cloned.1.call-done = bf16[384,4096]{1,0:T(8,128)(2,1)} async-done(((bf16[24,4096]{1,0:T(8,128)(2,1)}), bf16[384,4096]{1,0:T(8,128)(2,1)}) %all-gather.3.cloned.1.call-update) | async-done | bytes 3145744 | tf_op jit(solution)/shard_map/all_gather | solution.py:30
  86.2 8.9 %multiply_convert_fusion.1 = (bf16[384,924]{0,1:T(8,128)(2,1)S(1)}, bf16[384,924]{0,1:T(8,128)(2,1)S(1)}) fusion(f32[384,924]{0,1:T(8,128)S(1)} %fusion.11, f32[384,924]{0,1:T(8,128)} %fusion.10, bf16[384,4096]{1,0:T(8,128)(2,1)} %all-gather.3.cloned.1.call-done, bf16[924,4096]{1,0:T(8,128)(2,1)} %param.10), kind=kOutput, calls=%fused_computation.5 | convolution fusion | flops 2911265280 | bytes 14972928 | tf_op jit(solution)/shard_map/dot_general | solution.py:14
  95.1 5.8 %fusion.12 = f32[384,4096]{1,0:T(8,128)S(1)} fusion(bf16[384,924]{0,1:T(8,128)(2,1)S(1)} %get-tuple-element.8, bf16[4096,924]{0,1:T(8,128)(2,1)} %param.8), kind=kOutput, calls=%fused_computation.26 | convolution fusion | flops 2906652672 | bytes 14570496 | tf_op jit(solution)/shard_map/dot_general | solution.py:14
  101.0 8.5 %add_convert_fusion = bf16[384,4096]{1,0:T(8,128)(2,1)} fusion(f32[384,4096]{1,0:T(8,128)S(1)} %fusion.12, bf16[384,924]{0,1:T(8,128)(2,1)S(1)} %get-tuple-element.7, bf16[4096,924]{0,1:T(8,128)(2,1)} %param.9), kind=kOutput, calls=%fused_computation.3 | convolution fusion | flops 2909798400 | bytes 17716224 | tf_op jit(solution)/shard_map/dot_general | solution.py:14
  109.5 0.0 reduce-scatter.5.cloned.1.call-update
  109.5 0.2 reduce-scatter.11.cloned.1.call-start
  109.8 9.5 %convolution_convert_fusion = bf16[924,4096]{1,0:T(8,128)(2,1)} fusion(bf16[384,4096]{1,0:T(8,128)(2,1)} %all-gather.3.cloned.1.call-done, f32[384,924]{0,1:T(8,128)} %fusion.10, f32[384,924]{0,1:T(8,128)S(1)} %fusion.11), kind=kOutput, calls=%fused_computation | convolution fusion | flops 2912566272 | bytes 13553664 | tf_op jit(solution)/shard_map/dot_general | solution.py:8
  119.3 0.0 reduce-scatter.11.cloned.1.call-update
  119.3 0.0 reduce-scatter.9.cloned.1.call-start
  119.3 8.1 %convolution_convert_fusion.1 = bf16[4096,924]{0,1:T(8,128)(2,1)} fusion(bf16[384,4096]{1,0:T(8,128)(2,1)} %all-gather.5.cloned.1.call-done, bf16[384,924]{0,1:T(8,128)(2,1)S(1)} %get-tuple-element.7), kind=kOutput, calls=%fused_computation.1 | convolution fusion | flops 2910437376 | bytes 11424768 | tf_op jit(solution)/shard_map/dot_general | solution.py:8
  127.4 0.0 reduce-scatter.9.cloned.1.call-update
  127.5 0.0 reduce-scatter.7.cloned.1.call-start
  127.5 8.1 %convolution_convert_fusion.2 = bf16[4096,924]{0,1:T(8,128)(2,1)} fusion(bf16[384,4096]{1,0:T(8,128)(2,1)} %all-gather.5.cloned.1.call-done, bf16[384,924]{0,1:T(8,128)(2,1)S(1)} %get-tuple-element.8), kind=kOutput, calls=%fused_computation.2 | convolution fusion | flops 2910437376 | bytes 11424768 | tf_op jit(solution)/shard_map/dot_general | solution.py:8
  135.6 0.0 copy-start
  135.6 0.0 copy-start.1
  135.6 0.0 reduce-scatter.7.cloned.1.call-update
  135.6 39.8 %reduce-scatter.5.cloned.1.call-done = bf16[24,4096]{1,0:T(8,128)(2,1)} async-done(((bf16[384,4096]{1,0:T(8,128)(2,1)}), bf16[24,4096]{1,0:T(8,128)(2,1)}) %reduce-scatter.5.cloned.1.call-update) | async-done | bytes 196624 | tf_op jit(solution)/shard_map/reduce_scatter | solution.py:41
  175.4 0.0 copy-done
  175.4 0.0 copy-done.1
  175.5 1.2 fusion.7
  176.7 81.0 %psum.7 = f32[4096]{0:T(1024)} all-reduce(f32[4096]{0:T(1024)S(1)} %get-tuple-element.5), channel_id=1, replica_groups=mesh['dp'=8,'tensor'=16] {'dp','tensor'}, use_global_device_ids=true, to_apply=%region_4.0 | all-reduce | flops 4096 | bytes 32768 | tf_op jit(solution)/shard_map/psum | solution.py:49
  257.7 1.8 fusion.5
  259.4 30.6 %reduce-scatter.11.cloned.1.call-done = bf16[924,512]{1,0:T(8,128)(2,1)} async-done(((bf16[924,4096]{1,0:T(8,128)(2,1)}), bf16[924,512]{1,0:T(8,128)(2,1)}) %reduce-scatter.11.cloned.1.call-update) | async-done | bytes 946192 | tf_op jit(solution)/shard_map/reduce_scatter | solution.py:60
  290.0 113.4 %reduce-scatter.9.cloned.1.call-done = bf16[512,924]{0,1:T(8,128)(2,1)} async-done(((bf16[4096,924]{0,1:T(8,128)(2,1)}), bf16[512,924]{0,1:T(8,128)(2,1)}) %reduce-scatter.9.cloned.1.call-update) | async-done | bytes 946192 | tf_op jit(solution)/shard_map/reduce_scatter | solution.py:57
  403.4 113.0 %reduce-scatter.7.cloned.1.call-done = bf16[512,924]{0,1:T(8,128)(2,1)} async-done(((bf16[4096,924]{0,1:T(8,128)(2,1)}), bf16[512,924]{0,1:T(8,128)(2,1)}) %reduce-scatter.7.cloned.1.call-update) | async-done | bytes 946192 | tf_op jit(solution)/shard_map/reduce_scatter | solution.py:54
  (2 shorter events, 0.0 us)
Async XLA Ops:
  7.2 41.3 %all-gather.5.cloned.1.call-start = ((), (), s32[]{:S(2)}) async-start(), calls=%async_computation.5 | async-start | bytes 3342336 | tf_op jit(solution)/shard_map/all_gather | solution.py:29
  10.1 76.1 %all-gather.3.cloned.1.call-start = ((), (), s32[]{:S(2)}) async-start(), calls=%async_computation.4 | async-start | bytes 3342336 | tf_op jit(solution)/shard_map/all_gather | solution.py:30
  10.8 164.6 %reduce-scatter.5.cloned.1.call-start = ((), (), s32[]{:S(2)}) async-start(), calls=%async_computation.6 | async-start | bytes 3342336 | tf_op jit(solution)/shard_map/reduce_scatter | solution.py:41
  48.5 8.2 %copy-start.2 = (bf16[384,4096]{1,0:T(8,128)(2,1)S(1)}, bf16[384,4096]{1,0:T(8,128)(2,1)}, u32[]{:S(2)}) copy-start(bf16[384,4096]{1,0:T(8,128)(2,1)} %all-gather.5.cloned.1.call-done) | copy-start | bytes 9437188
  109.5 180.5 %reduce-scatter.11.cloned.1.call-start = ((), (), s32[]{:S(2)}) async-start(), calls=%async_computation.9 | async-start | bytes 8552448 | tf_op jit(solution)/shard_map/reduce_scatter | solution.py:60
  119.3 284.1 %reduce-scatter.9.cloned.1.call-start = ((), (), s32[]{:S(2)}) async-start(), calls=%async_computation.8 | async-start | bytes 8552448 | tf_op jit(solution)/shard_map/reduce_scatter | solution.py:57
  127.5 389.0 %reduce-scatter.7.cloned.1.call-start = ((), (), s32[]{:S(2)}) async-start(), calls=%async_computation.7 | async-start | bytes 8552448 | tf_op jit(solution)/shard_map/reduce_scatter | solution.py:54
  135.6 39.8 %copy-start = (bf16[24,4096]{1,0:T(8,128)(2,1)S(1)}, bf16[24,4096]{1,0:T(8,128)(2,1)}, u32[]{:S(2)}) copy-start(bf16[24,4096]{1,0:T(8,128)(2,1)} %param.6) | copy-start | bytes 589828
  135.6 39.8 %copy-start.1 = (f32[4096]{0:T(1024)S(1)}, f32[4096]{0:T(1024)}, u32[]{:S(2)}) copy-start(f32[4096]{0:T(1024)} %param.7) | copy-start | bytes 49156
Sparse Core Ops, SparseCore 0:
  10.3 38.1 all-gather.4
  50.2 35.9 all-gather.2
  109.6 65.7 reduce-scatter.4
  179.8 110.1 reduce-scatter.10
  294.9 108.5 reduce-scatter.8
  407.8 108.5 reduce-scatter.6
where the time goes:
time: 524 us; the launch traced here: 523 us
  waiting for transfers between devices  357 us (68%)
  blocking collectives  81 us (15%)
  matrix products  64.7 us (12%)
  between operations  14.2 us (3%)
  other arithmetic  5.83 us (1%)
    reduce_scatter x1, waiting for transfers between devices, body(): lax.psum_scatter(up_term.astype(jnp.bfloat16), 'dp', scatter_dimension=0,...  113 us
    reduce_scatter x1, waiting for transfers between devices, body(): lax.psum_scatter(gate_term.astype(jnp.bfloat16), 'dp', scatter_dimension=...  113 us
    psum x1, blocking collectives, body(): lax.psum(jnp.sum(normalized_gradient * unit_input, axis=0), ('dp', 'tenso...  81 us
    reduce_scatter x1, waiting for transfers between devices, body(): lax.psum_scatter(partial_sum.astype(jnp.bfloat16), 'tensor', scatter_dime...  39.8 us
    all_gather x1, waiting for transfers between devices, body(): lax.all_gather(normed_rows, 'tensor', axis=0, tiled=True)  37.6 us
    reduce_scatter x1, waiting for transfers between devices, body(): lax.psum_scatter(down_term.astype(jnp.bfloat16), 'dp', scatter_dimension=...  30.6 us
    dot_general x3, matrix products, contract_rows(): lax.dot_general(left, right, (((0,), (0,)), ((), ())), preferred_element_...  25.7 us
    dot_general x3, matrix products, contract_cols(): lax.dot_general(left, right, (((1,), (1,)), ((), ())), preferred_element_...  23.3 us
  transfers between devices with their start and end apart: 6, of which 6 were waited for; matrix products, arithmetic and copies ran while one was open for 8% of the time, Pallas kernels for 0%

commit v1 on v0

v1 whole, which is shorter than its diff:
```python
import functools

import jax
import jax.numpy as jnp
from jax import lax
from jax.experimental import pallas as pl
from jax.experimental.pallas import tpu as pltpu
from jax.sharding import PartitionSpec as P

MESH = pl.DeviceIdType.MESH
BF = jnp.bfloat16
F32 = jnp.float32
D = 4096
HALF = 2048
QUART = 1024
ROWS = 48
PLANE = 768
GROUP = 384
BLK = 512
CORE_FF = 924
MAIN = 896
REM = CORE_FF - MAIN
NW = 2 * MAIN + 128
HW = 928
XW = NW + MAIN


def coords():
    dp = lax.axis_index("dp")
    t = lax.axis_index("tensor")
    y = dp // 2
    z = (dp % 2) * 2 + (t // 2) % 2
    return t // 4, y, z, t % 2


def device(x, y, z, c):
    x, y, z, c = (x + 4) % 4, (y + 4) % 4, (z + 4) % 4, (c + 2) % 2
    return (y * 2 + z // 2, x * 4 + (z % 2) * 2 + c)


def remote(src, dst, ss, rs, to):
    return pltpu.make_async_remote_copy(
        src_ref=src, dst_ref=dst, send_sem=ss, recv_sem=rs, device_id=to, device_id_type=MESH
    )


def greet(peers):
    barrier = pltpu.get_barrier_semaphore()
    for to in peers:
        pl.semaphore_signal(barrier, inc=1, device_id=to, device_id_type=MESH)
    pl.semaphore_wait(barrier, len(peers))


OFFS = (0, -1, 1, 2)


def slot(i, j):
    return (i % 4) * 4 + (j % 4)


def gather_kernel(
    li_ref, go_ref, gain_ref, n_ref, g_ref, other, ex_s, ex_r, s_sem, r_sem, c_s, c_r
):
    x, y, z, c = coords()
    core = device(x, y, z, 1 - c)
    step = {
        "x": (device(x + 1, y, z, c), device(x - 1, y, z, c)),
        "z": (device(x, y, z + 1, c), device(x, y, z - 1, c)),
    }
    greet([core, *step["x"], *step["z"]])
    swaps = []
    for a, ref in enumerate((li_ref, go_ref)):
        cp = remote(ref, other.at[a], ex_s.at[a], ex_r.at[a], core)
        cp.start()
        swaps.append(cp)

    base = pl.multiple_of((z * 4 + x) * ROWS, 16)
    first = c == 0
    outs = (n_ref, g_ref)

    swaps[0].wait_recv()
    scale = []
    for ref in (li_ref, other.at[0]):
        rows = ref[...].astype(F32)
        scale.append(jnp.sqrt(jnp.mean(rows * rows, axis=1, keepdims=True) + 1e-06))
    swaps[1].wait_recv()
    for k in range(8):
        cols = pl.ds(k * 512, 512)
        mine = (li_ref[:, cols].astype(F32) / scale[0]) * gain_ref[:, cols]
        theirs = (other[0, :, cols].astype(F32) / scale[1]) * gain_ref[:, cols]
        both = jnp.concatenate(
            [jnp.where(first, mine, theirs), jnp.where(first, theirs, mine)], axis=0
        )
        n_ref[pl.ds(base, ROWS), cols] = both.astype(BF)
        mine = go_ref[:, cols].astype(F32)
        theirs = other[1, :, cols].astype(F32)
        both = jnp.concatenate(
            [jnp.where(first, mine, theirs), jnp.where(first, theirs, mine)], axis=0
        )
        g_ref[pl.ds(base, ROWS), cols] = both.astype(BF)

    lo = pl.multiple_of(c * HALF, 128)
    wide = (pl.ds(lo, HALF), pl.ds(lo, QUART), pl.ds(pl.multiple_of(lo + QUART, 128), QUART))

    def block(a, i, j, part=0):
        if a == 0:
            zz, xx = (z + j + 4) % 4, (x + i + 4) % 4
        else:
            zz, xx = (z + i + 4) % 4, (x + j + 4) % 4
        return outs[a].at[pl.ds(pl.multiple_of((zz * 4 + xx) * ROWS, 16), ROWS), wide[part]]

    sent = []
    count = [0, 0]

    def push(a, leg, way, i, j, part=0):
        axis = ("x", "z")[(a + leg) % 2]
        to = step[axis][0 if way > 0 else 1]
        ri, rj = (i - way, j) if leg == 0 else (i, j - way)
        ref = block(a, i, j, part)
        k = 1 if part == 2 else 0
        cp = remote(ref, ref, s_sem.at[a, count[a]], r_sem.at[a, slot(ri, rj), k], to)
        count[a] += 1
        cp.start()
        sent.append(cp)

    def arrived(a, i, j):
        if i == 2 and j == 0 or j == 2:
            parts = (1, 2)
        else:
            parts = (0,)
        for part in parts:
            ref = block(a, i, j, part)
            k = 1 if part == 2 else 0
            remote(ref, ref, s_sem.at[a, 0], r_sem.at[a, slot(i, j), k], core).wait_recv()

    def share(a, i, j):
        ref = block(a, i, j)
        k = slot(i, j)
        cp = remote(ref, ref, c_s.at[a, k], c_r.at[a, k], core)
        cp.start()
        sent.append(cp)

    for a in (0, 1):
        for way in (1, -1):
            push(a, 0, way, 0, 0)
    for a in (0, 1):
        for way in (1, -1):
            push(a, 1, way, 0, 0)
    for a in (0, 1):
        for way in (1, -1):
            arrived(a, -way, 0)
            push(a, 0, way, -way, 0, 1 if way > 0 else 2)
            push(a, 1, 1, -way, 0)
            push(a, 1, -1, -way, 0)
            share(a, -way, 0)
    for i in OFFS:
        for a in (0, 1):
            if i == 2:
                arrived(a, 2, 0)
                push(a, 1, 1, 2, 0)
                push(a, 1, -1, 2, 0)
                share(a, 2, 0)
        for a in (0, 1):
            for way in (1, -1):
                arrived(a, i, -way)
                push(a, 1, way, i, -way, 1 if way > 0 else 2)
                share(a, i, -way)
    for i in OFFS:
        for a in (0, 1):
            arrived(a, i, 2)
            share(a, i, 2)

    theirs = pl.ds(pl.multiple_of((1 - c) * HALF, 128), HALF)
    for a in (0, 1):
        for i in OFFS:
            for j in OFFS:
                if (i, j) != (0, 0):
                    if a == 0:
                        zz, xx = (z + j + 4) % 4, (x + i + 4) % 4
                    else:
                        zz, xx = (z + i + 4) % 4, (x + j + 4) % 4
                    ref = outs[a].at[
                        pl.ds(pl.multiple_of((zz * 4 + xx) * ROWS, 16), ROWS), theirs
                    ]
                    k = slot(i, j)
                    remote(ref, ref, c_s.at[a, k], c_r.at[a, k], core).wait_recv()
    for cp in swaps + sent:
        cp.wait_send()


def gather(layer_input, grad_out, gain):
    vmem = pl.BlockSpec(memory_space=pltpu.VMEM)
    dma = pltpu.SemaphoreType.DMA
    return pl.pallas_call(
        gather_kernel,
        out_shape=[jax.ShapeDtypeStruct((PLANE, D), BF)] * 2,
        in_specs=[vmem] * 3,
        out_specs=[vmem] * 2,
        scratch_shapes=[
            pltpu.VMEM((2, 24, D), BF),
            dma((2,)),
            dma((2,)),
            dma((2, 20)),
            dma((2, 16, 2)),
            dma((2, 16)),
            dma((2, 16)),
        ],
        compiler_params=pltpu.CompilerParams(
            collective_id=0, has_side_effects=True, vmem_limit_bytes=48 << 20
        ),
    )(layer_input, grad_out, gain)


PART_A = (("n", 0, 512), ("n", 512, 512), ("h", 0, 400))
PART_B = (("n", 1024, 512), ("n", 1536, 384), ("h", 400, 528))
NC = len(PART_A)


def reduce_kernel(
    n_hbm, g_hbm, x_ref, p_ref, li_ref, gain_ref,
    tn_out, th_out, ig_out, gain_out,
    nb, gb, nt, ht, far_n, far_h, mid_n, mid_h, to_n, to_h, in_n, in_h, own_n, own_h,
    pc, q, xo, xi, xs, xr, zs, zr, dn, gs, gr,
    load, far_s, far_r, near_s, near_r, p_s, p_r, g_sem, g_rec,
):
    x, y, z, c = coords()
    zl, zh = z % 2, z // 2
    core = device(x, y, z, 1 - c)
    xs_dev = [device(x + k, y, z, c) for k in (1, -1, 2)]
    ys_dev = [device(x, y + k, z, c) for k in (1, -1, 2)]
    zs_dev = [device(x, y, z + k, c) for k in (1, -1, 2)]
    zpair = device(x, y, zh * 2 + 1 - zl, c)

    loads = {}
    for r in (2, 1, -1, 0):
        k = r % 4
        cols = pl.ds(pl.multiple_of((((y + r + 4) % 4) * 2 + zh) * BLK, 128), BLK)
        loads[r] = [
            pltpu.make_async_copy(n_hbm.at[:, cols], nb.at[k], load.at[0, k]),
            pltpu.make_async_copy(g_hbm.at[:, cols], gb.at[k], load.at[1, k]),
        ]
        for cp in loads[r]:
            cp.start()
    greet([core, *xs_dev, *ys_dev, *zs_dev])
    sent = []

    def send(src, dst, ss, rs, to):
        cp = remote(src, dst, ss, rs, to)
        cp.start()
        sent.append(cp)
        return cp

    mine = pl.ds(pl.multiple_of(c * HALF, 128), HALF)
    theirs = pl.ds(pl.multiple_of((1 - c) * HALF, 128), HALF)
    swap = send(p_ref.at[:, theirs], pc, p_s.at[0], p_r.at[0], core)

    ht[0:MAIN, :] = x_ref[:, NW:XW].T
    ht[MAIN:, :] = x_ref[:, NW - 128:NW].T

    def ready(r):
        for cp in loads[r]:
            cp.wait()
        nt[r % 4] = nb[r % 4].T

    def term(r, chunk):
        kind, s, w = chunk
        if kind == "n":
            return jnp.dot(nt[r % 4], x_ref[:, s:s + w], preferred_element_type=F32)
        return jnp.dot(ht[s:s + w, :], gb[r % 4], preferred_element_type=F32)

    def view(n, h, chunk):
        kind, s, w = chunk
        return n.at[:, pl.ds(s, w)] if kind == "n" else h.at[pl.ds(s, w), :]

    ready(2)
    for k in range(NC):
        for part, chunk in enumerate((PART_A[k], PART_B[k])):
            ref = view(far_n, far_h, chunk)
            ref[...] = term(2, chunk).astype(BF)
            send(
                ref, view(mid_n, mid_h, chunk), far_s.at[part, k], far_r.at[part, k],
                ys_dev[part],
            )

    def near(part, chunk, k, which, extra):
        r = 1 if part == 0 else -1
        value = term(r, chunk)
        if extra:
            value = value + view(mid_n, mid_h, chunk)[...].astype(F32)
        ref = view(to_n.at[part], to_h.at[part], chunk)
        ref[...] = value.astype(BF)
        send(
            ref, view(in_n.at[part], in_h.at[part], chunk),
            near_s.at[part, which, k], near_r.at[part, which, k], ys_dev[part],
        )

    ready(1)
    ready(-1)
    for k in range(NC):
        near(0, PART_B[k], k, 1, False)
        near(1, PART_A[k], k, 0, False)
    ready(0)
    for k in range(NC):
        for chunk in (PART_A[k], PART_B[k]):
            view(own_n, own_h, chunk)[...] = term(0, chunk)

    swap.wait_recv()
    q[...] = p_ref[:, mine].astype(F32) + pc[...].astype(F32)

    def rows_of(zz, xx):
        return pl.ds(pl.multiple_of((zz * 4 + (xx + 4) % 4) * ROWS, 16), ROWS)

    for zz in (0, 1):
        xo[zz * ROWS:(zz + 1) * ROWS, :] = q[rows_of(zz, x + 2), :].astype(BF)
    far = [
        send(
            xo.at[:, pl.ds(k * QUART, QUART)], xi.at[:, pl.ds(k * QUART, QUART)],
            p_s.at[1 + k], p_r.at[1 + k], xs_dev[k],
        )
        for k in (0, 1)
    ]
    step = []
    for k in (0, 1):
        far[k].wait_recv()
        for zz in (0, 1):
            rows = pl.ds(zz * ROWS, ROWS)
            src = rows_of(zz, x + (1 if k == 0 else -1))
            for half in (0, 1):
                cols = pl.ds(half * QUART, QUART)
                value = q[src, cols]
                if half == k:
                    value = value + xi[rows, cols].astype(F32)
                xs[k, rows, cols] = value.astype(BF)
        step.append(send(xs.at[k], xr.at[k], p_s.at[3 + k], p_r.at[3 + k], xs_dev[k]))
    for k in (0, 1):
        step[k].wait_recv()

    def summed(zz):
        rows = pl.ds(pl.multiple_of(zz * ROWS, 16), ROWS)
        return q[rows_of(zz, x), :] + xr[0, rows, :].astype(F32) + xr[1, rows, :].astype(F32)

    zs[...] = summed(1 - zl).astype(BF)
    hop = send(zs, zr, p_s.at[5], p_r.at[5], zpair)
    hop.wait_recv()
    q[0:ROWS, :] = summed(zl) + zr[...].astype(F32)
    dn[:, mine] = q[pl.ds(pl.multiple_of(c * 24, 8), 24), :]
    last = send(
        q.at[pl.ds(pl.multiple_of((1 - c) * 24, 8), 24), :], dn.at[:, mine],
        p_s.at[6], p_r.at[6], core,
    )
    last.wait_recv()

    inputs = li_ref[...].astype(F32)
    rms = jnp.sqrt(jnp.mean(inputs * inputs, axis=1, keepdims=True) + 1e-06)
    unit = inputs / rms
    scaled = gain_ref[...] * dn[...]
    inner = jnp.mean(scaled * unit, axis=1, keepdims=True)
    ig_out[...] = ((scaled - unit * inner) / rms).astype(BF)
    total = jnp.sum(dn[...] * unit, axis=0, keepdims=True)
    for s, peers in enumerate(([core], xs_dev, zs_dev, ys_dev)):
        gs[s] = total
        cps = []
        for k, to in enumerate(peers):
            cps.append(send(gs.at[s], gr.at[s, k], g_sem.at[s, k], g_rec.at[s, k], to))
        for k, cp in enumerate(cps):
            cp.wait_recv()
            total = total + gr[s, k]
    gain_out[...] = total

    for k in range(NC):
        for part, chunk in enumerate((PART_A[k], PART_B[k])):
            ref = view(mid_n, mid_h, chunk)
            remote(ref, ref, far_s.at[part, k], far_r.at[part, k], core).wait_recv()
            near(part, chunk, k, part, True)

    for which, parts in ((0, PART_A), (1, PART_B)):
        for k in range(NC):
            chunk = parts[k]
            value = view(own_n, own_h, chunk)[...]
            for part in (0, 1):
                ref = view(in_n.at[part], in_h.at[part], chunk)
                remote(
                    ref, ref, near_s.at[part, which, k], near_r.at[part, which, k], core
                ).wait_recv()
                value = value + ref[...].astype(F32)
            view(tn_out, th_out, chunk)[...] = value.astype(BF)
    for cp in sent:
        cp.wait_send()


def reduce(n, g, xp, p, layer_input, gain):
    vmem = pl.BlockSpec(memory_space=pltpu.VMEM)
    hbm = pl.BlockSpec(memory_space=pl.ANY)
    dma = pltpu.SemaphoreType.DMA
    v = pltpu.VMEM
    return pl.pallas_call(
        reduce_kernel,
        out_shape=[
            jax.ShapeDtypeStruct((BLK, NW), BF),
            jax.ShapeDtypeStruct((HW, BLK), BF),
            jax.ShapeDtypeStruct((24, D), BF),
            jax.ShapeDtypeStruct((1, D), F32),
        ],
        in_specs=[hbm, hbm, vmem, vmem, vmem, vmem],
        out_specs=[vmem] * 4,
        scratch_shapes=[
            v((4, PLANE, BLK), BF),
            v((4, PLANE, BLK), BF),
            v((4, BLK, PLANE), BF),
            v((MAIN + 128, PLANE), BF),
            v((BLK, NW), BF),
            v((HW, BLK), BF),
            v((BLK, NW), BF),
            v((HW, BLK), BF),
            v((2, BLK, NW), BF),
            v((2, HW, BLK), BF),
            v((2, BLK, NW), BF),
            v((2, HW, BLK), BF),
            v((BLK, NW), F32),
            v((HW, BLK), F32),
            v((GROUP, HALF), BF),
            v((GROUP, HALF), F32),
            v((2 * ROWS, HALF), BF),
            v((2 * ROWS, HALF), BF),
            v((2, 2 * ROWS, HALF), BF),
            v((2, 2 * ROWS, HALF), BF),
            v((ROWS, HALF), BF),
            v((ROWS, HALF), BF),
            v((24, D), F32),
            v((4, 1, D), F32),
            v((4, 3, 1, D), F32),
            dma((2, 4)),
            dma((2, NC)),
            dma((2, NC)),
            dma((2, 2, NC)),
            dma((2, 2, NC)),
            dma((7,)),
            dma((7,)),
            dma((4, 3)),
            dma((4, 3)),
        ],
        compiler_params=pltpu.CompilerParams(
            collective_id=1, has_side_effects=True, vmem_limit_bytes=60 << 20
        ),
    )(n, g, xp, p, layer_input, gain)


def contract_cols(left, right):
    return lax.dot_general(left, right, (((1,), (1,)), ((), ())), preferred_element_type=F32)


def body(layer_input, gain_vector, w_gate, w_up, w_down, grad_out):
    gain = gain_vector[None, :]
    normed, upstream = gather(layer_input, grad_out, gain)
    gate = jnp.dot(normed, w_gate, preferred_element_type=F32)
    up = jnp.dot(normed, w_up, preferred_element_type=F32)
    sigma = jax.nn.sigmoid(gate)
    silu = gate * sigma
    hidden = (silu * up).astype(BF)
    d_hidden = contract_cols(upstream, w_down)
    d_gate = (d_hidden * up * sigma * (1.0 + gate * (1.0 - sigma))).astype(BF)
    d_up = (d_hidden * silu).astype(BF)
    start = (lax.axis_index("dp") % 2) * GROUP
    own_gate = lax.dynamic_slice_in_dim(d_gate, start, GROUP, 0)
    own_up = lax.dynamic_slice_in_dim(d_up, start, GROUP, 0)
    share = (contract_cols(own_gate, w_gate) + contract_cols(own_up, w_up)).astype(BF)
    packed = jnp.concatenate(
        [
            d_gate[:, :MAIN],
            d_up[:, :MAIN],
            hidden[:, MAIN:],
            d_gate[:, MAIN:],
            d_up[:, MAIN:],
            jnp.zeros((PLANE, 128 - 3 * REM), BF),
            hidden[:, :MAIN],
        ],
        axis=1,
    )
    tn, th, input_gradient, gain_gradient = reduce(
        normed, upstream, packed, share, layer_input, gain
    )
    rest = 2 * MAIN + REM
    return (
        input_gradient,
        gain_gradient[0],
        jnp.concatenate([tn[:, :MAIN], tn[:, rest:rest + REM]], axis=1),
        jnp.concatenate([tn[:, MAIN:2 * MAIN], tn[:, rest + REM:rest + 2 * REM]], axis=1),
        th[:CORE_FF],
    )


def solution(mesh):
    return jax.shard_map(
        body,
        mesh=mesh,
        in_specs=(
            P(("dp", "tensor"), None),
            P(),
            P(None, "tensor"),
            P(None, "tensor"),
            P("tensor", None),
            P(("dp", "tensor"), None),
        ),
        out_specs=(
            P(("dp", "tensor"), None),
            P(),
            P("dp", "tensor"),
            P("dp", "tensor"),
            P("tensor", "dp"),
        ),
        check_vma=False,
    )
```

time: 524 us -> 224 us (0.43)
  waiting for transfers between devices: 357 us -> 0 us
  Pallas kernels: 0 us -> 161 us
  blocking collectives: 81 us -> 0 us
  matrix products: 64.7 us -> 41.2 us
  local copies, waits for them, and re-layouts: 0.01 us -> 19.7 us
  between operations: 14.2 us -> 0.85 us
  other arithmetic: 5.83 us -> 0.31 us
    reduce_scatter x4 -> x0, waiting for transfers between devices: 297 us -> none  [the longest x1 113 us: body(): lax.psum_scatter(up_term.astype(jnp.bfloat16), 'dp', scatter_dimension=0,...]
    pallas_call x0 -> x2, Pallas kernels: none -> 161 us  [the longest x1 111 us: reduce(): pl.pallas_call(reduce_kernel, out_shape=[jax.ShapeDtypeStruct((BLK, NW),...]
    psum x1 -> x0, blocking collectives: 81 us -> none  [body(): lax.psum(jnp.sum(normalized_gradient * unit_input, axis=0), ('dp', 'tenso...]
    all_gather x2 -> x0, waiting for transfers between devices: 59.6 us -> none  [the longest x1 37.6 us: body(): lax.all_gather(normed_rows, 'tensor', axis=0, tiled=True)]
    dot_general x5 -> x2, matrix products: 41.4 us -> 22.1 us  [the longest x1 11.1 us: body(): gate = jnp.dot(normed, w_gate, preferred_element_type=F32)]
    concatenate x0 -> x1, local copies, waits for them, and re-layouts: none -> 7.9 us  [body(): jnp.concatenate([d_gate[:, :MAIN], d_up[:, :MAIN], hidden[:, MAIN:], d_ga...]
    unnamed x6 -> x27, local copies, waits for them, and re-layouts: 0.01 us -> 7.39 us
  transfers between devices with their start and end apart: 6 -> 0, of which waited for: 6 -> 0; matrix products, arithmetic and copies ran while one was open for 8% -> 0% of each run, Pallas kernels for 0% -> 0%
where the time goes in v1:
time: 224 us; the launch traced here: 223 us
  Pallas kernels  161 us (72%)
  matrix products  41.2 us (18%)
  local copies, waits for them, and re-layouts  19.7 us (9%)
    pallas_call x1, Pallas kernels, reduce(): pl.pallas_call(reduce_kernel, out_shape=[jax.ShapeDtypeStruct((BLK, NW),...  111 us
    pallas_call x1, Pallas kernels, gather(): pl.pallas_call(gather_kernel, out_shape=[jax.ShapeDtypeStruct((PLANE, D),...  49.9 us
    dot_general x3, matrix products, contract_cols(): lax.dot_general(left, right, (((1,), (1,)), ((), ())), preferred_element_...  19.1 us
    dot_general x1, matrix products, body(): gate = jnp.dot(normed, w_gate, preferred_element_type=F32)  11.1 us
    dot_general x1, matrix products, body(): up = jnp.dot(normed, w_up, preferred_element_type=F32)  11 us
    concatenate x1, local copies, waits for them, and re-layouts, body(): jnp.concatenate([d_gate[:, :MAIN], d_up[:, :MAIN], hidden[:, MAIN:], d_ga...  7.9 us
    unnamed x27, local copies, waits for them, and re-layouts  7.39 us

profile of v1, /device:TPU:0, one launch (start us, length us, event | category | flops | bytes accessed | tf_op | source)
XLA Modules:
  0.0 223.1 jit_solution(9993967793016852044)
XLA Ops:
  0.6 0.0 copy-start
  0.7 0.9 copy-done
  1.6 0.0 copy-start.1
  1.6 0.9 copy-done.1
  2.5 0.0 copy-start.2
  2.5 0.7 copy-done.2
  3.2 49.9 %shard_map.101 = (bf16[768,4096]{1,0:T(8,128)(2,1)}, bf16[768,4096]{1,0:T(8,128)(2,1)}) custom-call(bf16[24,4096]{1,0:T(8,128)(2,1)S(1)} %copy-done, bf16[24,4096]{1,0:T(8,128)(2,1)S(1)} %copy-done.1, f32[1,4096]{1,0:T(1,128)S(1)} %bitcast.12), custom_call_target="tpu_custom_call" | custom-call | tf_op jit(solution)/shard_map/pallas_call | solution.py:194
  53.1 0.0 copy-start.3
  53.1 0.0 copy-start.7
  53.1 0.0 slice-start
  53.2 11.1 %fusion.9 = f32[768,924]{1,0:T(8,128)S(1)} fusion(bf16[768,4096]{1,0:T(8,128)(2,1)} %get-tuple-element.11.n_hbm, bf16[4096,924]{0,1:T(8,128)(2,1)} %param.8), kind=kOutput, calls=%fused_computation.16 | convolution fusion | flops 5813305344 | bytes 16699392 | tf_op jit(solution)/shard_map/dot_general | solution.py:455
  64.3 0.0 slice-start.1
  64.3 0.0 copy-done.3
  64.3 0.0 copy-done.7
  64.3 8.3 %fusion.8 = f32[768,924]{1,0:T(8,128)} fusion(bf16[768,4096]{1,0:T(8,128)(2,1)S(1)} %copy-done.3, bf16[924,4096]{1,0:T(8,128)(2,1)S(1)} %copy-done.7), kind=kOutput, calls=%fused_computation.15 | convolution fusion | flops 5813305344 | bytes 16699392 | tf_op jit(solution)/shard_map/dot_general | solution.py:449
  72.7 0.0 slice-done
  72.7 0.0 slice-done.1
  72.7 11.0 %multiply_convert_fusion = (bf16[768,924]{1,0:T(8,128)(2,1)S(1)}, bf16[768,924]{1,0:T(8,128)(2,1)S(1)}, bf16[768,924]{1,0:T(8,128)(2,1)S(1)}) fusion(f32[768,924]{1,0:T(8,128)S(1)} %fusion.9, f32[768,924]{1,0:T(8,128)} %fusion.8, bf16[768,4096]{1,0:T(8,128)(2,1)S(1)} %bitcast.14, bf16[4096,924]{0,1:T(8,128)(2,1)} %param.9), kind=kOutput, calls=%fused_computation.1 | convolution fusion | flops 5823949824 | bytes 23795712 | tf_op jit(solution)/shard_map/dot_general | solution.py:456
  83.6 0.0 copy-start.8
  83.7 5.9 %fusion.2 = f32[384,4096]{1,0:T(8,128)S(1)} fusion(bf16[4096,924]{0,1:T(8,128)(2,1)} %param.8, bf16[768,924]{1,0:T(8,128)(2,1)S(1)} %get-tuple-element.23, s32[]{:T(128)S(6)} %select_n.12), kind=kOutput, calls=%fused_computation.9 | convolution fusion | flops 2906652672 | bytes 14647300 | tf_op jit(solution)/shard_map/dot_general | solution.py:449
  89.5 0.0 copy-done.8
  89.5 4.9 %add_convert_fusion.p_ref = bf16[384,4096]{1,0:T(8,128)(2,1)} fusion(f32[384,4096]{1,0:T(8,128)S(1)} %fusion.2, bf16[4096,924]{0,1:T(8,128)(2,1)S(1)} %copy-done.8, bf16[768,924]{1,0:T(8,128)(2,1)S(1)} %get-tuple-element.24, s32[]{:T(128)S(6)} %select_n.12), kind=kOutput, calls=%fused_computation | convolution fusion | flops 2909798400 | bytes 17825796 | tf_op jit(solution)/shard_map/dot_general | solution.py:449
  94.4 0.1 slice.44
  94.6 0.1 slice.45
  94.7 0.1 slice.47
  94.7 0.1 slice.48
  94.8 1.2 slice.49
  96.0 0.1 slice.46
  96.1 7.9 %concatenate.9.x_ref = bf16[768,2816]{1,0:T(8,128)(2,1)} concatenate(bf16[768,896]{1,0:T(8,128)(2,1)S(1)} %slice.44, bf16[768,896]{1,0:T(8,128)(2,1)S(1)} %slice.45, bf16[768,28]{1,0:T(8,128)(2,1)S(1)} %slice.46, bf16[768,28]{1,0:T(8,128)(2,1)S(1)} %slice.47, bf16[768,28]{1,0:T(8,128)(2,1)S(1)} %slice.48, bf16[768,44]{1,0:T(8,128)(2,1)S(1)} %broadcast_in_dim.7, ...), dimensions={1} | concatenate | bytes 8650752 | tf_op jit(solution)/shard_map/concatenate | solution.py:467
  104.0 111.2 %shard_map.102 = (bf16[512,1920]{1,0:T(8,128)(2,1)}, bf16[928,512]{1,0:T(8,128)(2,1)}, bf16[24,4096]{1,0:T(8,128)(2,1)}, f32[1,4096]{1,0:T(1,128)}) custom-call(bf16[768,4096]{1,0:T(8,128)(2,1)} %get-tuple-element.11.n_hbm, bf16[768,4096]{1,0:T(8,128)(2,1)} %get-tuple-element.12.g_hbm, bf16[768,2816]{1,0:T(8,128)(2,1)} %concatenate.9.x_ref, ...), custom_call_target="tpu_custom_call" | custom-call | tf_op jit(solution)/shard_map/pallas_call | solution.py:396
  215.2 1.6 fusion.6
  216.8 1.1 fusion.7
  217.9 0.0 copy-start.5
  217.9 0.3 pad_maximum_fusion
  218.3 0.0 copy-start.6
  218.3 0.0 copy-start.4
  218.3 1.3 copy.18
  219.6 1.3 copy.19
  220.8 0.0 copy-done.5
  220.8 0.7 copy.26
  221.5 0.0 copy-done.6
  221.5 0.6 copy.27
  222.1 0.0 copy-done.4
  222.1 0.9 copy.28
  (2 shorter events, 0.0 us)
Async XLA Ops:
  0.6 0.9 copy-start
  1.6 0.9 copy-start.1
  2.5 0.7 copy-start.2
  53.1 11.2 %copy-start.3 = (bf16[768,4096]{1,0:T(8,128)(2,1)S(1)}, bf16[768,4096]{1,0:T(8,128)(2,1)}, u32[]{:S(2)}) copy-start(bf16[768,4096]{1,0:T(8,128)(2,1)} %get-tuple-element.12.g_hbm) | copy-start | bytes 18874372
  53.1 11.2 %copy-start.7 = (bf16[924,4096]{1,0:T(8,128)(2,1)S(1)}, bf16[924,4096]{1,0:T(8,128)(2,1)}, u32[]{:S(2)}) copy-start(bf16[924,4096]{1,0:T(8,128)(2,1)} %param.10) | copy-start | bytes 22708228
  53.1 19.5 %slice-start = ((s8[6291456]{0:T(1024)(128)(4,1)}), s8[4194304]{0:T(1024)(128)(4,1)S(1)}, s32[]{:S(2)}) async-start(s8[6291456]{0:T(1024)(128)(4,1)} %bitcast.13), calls=%async_computation | async-start | bytes 8388608
  64.3 8.4 %slice-start.1 = ((s8[6291456]{0:T(1024)(128)(4,1)}), s8[2097152]{0:T(1024)(128)(4,1)S(1)}, s32[]{:S(2)}) async-start(s8[6291456]{0:T(1024)(128)(4,1)} %bitcast.13), calls=%async_computation.1 | async-start | bytes 4194304
  83.6 5.9 %copy-start.8 = (bf16[4096,924]{0,1:T(8,128)(2,1)S(1)}, bf16[4096,924]{0,1:T(8,128)(2,1)}, u32[]{:S(2)}) copy-start(bf16[4096,924]{0,1:T(8,128)(2,1)} %param.9) | copy-start | bytes 22708228
  217.9 2.9 %copy-start.5 = (bf16[24,4096]{1,0:T(8,128)(2,1)S(1)}, bf16[24,4096]{1,0:T(8,128)(2,1)}, u32[]{:S(2)}) copy-start(bf16[24,4096]{1,0:T(8,128)(2,1)} %get-tuple-element.36) | copy-start | bytes 589828
  218.3 3.3 %copy-start.6 = (f32[1,4096]{1,0:T(1,128)S(1)}, f32[1,4096]{1,0:T(1,128)}, u32[]{:S(2)}) copy-start(f32[1,4096]{1,0:T(1,128)} %get-tuple-element.14) | copy-start | bytes 49156
  218.3 3.9 %copy-start.4 = (bf16[928,512]{1,0:T(8,128)(2,1)S(1)}, bf16[928,512]{1,0:T(8,128)(2,1)}, u32[]{:S(2)}) copy-start(bf16[928,512]{1,0:T(8,128)(2,1)} %get-tuple-element.16) | copy-start | bytes 2850820

commit v2 on v1

--- a/solution.py
+++ b/solution.py
@@ -20,9 +20,8 @@
 CORE_FF = 924
 MAIN = 896
 REM = CORE_FF - MAIN
-NW = 2 * MAIN + 128
-HW = 928
-XW = NW + MAIN
+XW = 3 * MAIN + 128
+TR = 3 * MAIN + 96
 
 
 def coords():
@@ -52,27 +51,41 @@
 
 
 OFFS = (0, -1, 1, 2)
+PIECES = ((0, 256), (256, 256), (512, 256), (768, 156))
 
 
 def slot(i, j):
     return (i % 4) * 4 + (j % 4)
 
 
+def contract_cols(left, right):
+    return lax.dot_general(left, right, (((1,), (1,)), ((), ())), preferred_element_type=F32)
+
+
 def gather_kernel(
-    li_ref, go_ref, gain_ref, n_ref, g_ref, other, ex_s, ex_r, s_sem, r_sem, c_s, c_r
+    li_ref, go_ref, gain_ref, wg_hbm, wu_hbm, wd_hbm, n_hbm, g_hbm, x_hbm, p_hbm,
+    n_ref, g_ref, x_ref, dg_ref, du_ref, p_ref, wg, wu, wd, other,
+    w_sem, out_sem, ex_s, ex_r, s_sem, r_sem, c_s, c_r,
 ):
     x, y, z, c = coords()
+    s = 1 - 2 * (z % 2)
     core = device(x, y, z, 1 - c)
     step = {
         "x": (device(x + 1, y, z, c), device(x - 1, y, z, c)),
-        "z": (device(x, y, z + 1, c), device(x, y, z - 1, c)),
+        "z": (device(x, y, z + s, c), device(x, y, z - s, c)),
     }
+    weights = [
+        pltpu.make_async_copy(src, dst, w_sem.at[k])
+        for k, (src, dst) in enumerate(((wg_hbm, wg), (wu_hbm, wu), (wd_hbm, wd)))
+    ]
     greet([core, *step["x"], *step["z"]])
     swaps = []
     for a, ref in enumerate((li_ref, go_ref)):
         cp = remote(ref, other.at[a], ex_s.at[a], ex_r.at[a], core)
         cp.start()
         swaps.append(cp)
+    for cp in weights:
+        cp.start()
 
     base = pl.multiple_of((z * 4 + x) * ROWS, 16)
     first = c == 0
@@ -101,13 +114,15 @@
 
     lo = pl.multiple_of(c * HALF, 128)
     wide = (pl.ds(lo, HALF), pl.ds(lo, QUART), pl.ds(pl.multiple_of(lo + QUART, 128), QUART))
+    theirs = pl.ds(pl.multiple_of((1 - c) * HALF, 128), HALF)
+
+    def place(a, i, j):
+        dz, dx = (j, i) if a == 0 else (i, j)
+        zz, xx = (z + s * dz + 4) % 4, (x + dx + 4) % 4
+        return pl.ds(pl.multiple_of((zz * 4 + xx) * ROWS, 16), ROWS)
 
     def block(a, i, j, part=0):
-        if a == 0:
-            zz, xx = (z + j + 4) % 4, (x + i + 4) % 4
-        else:
-            zz, xx = (z + i + 4) % 4, (x + j + 4) % 4
-        return outs[a].at[pl.ds(pl.multiple_of((zz * 4 + xx) * ROWS, 16), ROWS), wide[part]]
+        return outs[a].at[place(a, i, j), wide[part]]
 
     sent = []
     count = [0, 0]
@@ -115,7 +130,9 @@
     def push(a, leg, way, i, j, part=0):
         axis = ("x", "z")[(a + leg) % 2]
         to = step[axis][0 if way > 0 else 1]
-        ri, rj = (i - way, j) if leg == 0 else (i, j - way)
+        at = (i, j)[leg]
+        at = at - way if axis == "x" else way - at
+        ri, rj = (at, j) if leg == 0 else (i, at)
         ref = block(a, i, j, part)
         k = 1 if part == 2 else 0
         cp = remote(ref, ref, s_sem.at[a, count[a]], r_sem.at[a, slot(ri, rj), k], to)
@@ -123,17 +140,18 @@
         cp.start()
         sent.append(cp)
 
-    def arrived(a, i, j):
-        if i == 2 and j == 0 or j == 2:
-            parts = (1, 2)
-        else:
-            parts = (0,)
-        for part in parts:
+    def arrive(a, i, j):
+        for part in (1, 2) if (i, j) == (2, 0) or j == 2 else (0,):
             ref = block(a, i, j, part)
             k = 1 if part == 2 else 0
             remote(ref, ref, s_sem.at[a, 0], r_sem.at[a, slot(i, j), k], core).wait_recv()
-
-    def share(a, i, j):
+        if j == 0:
+            if i in (1, -1):
+                push(a, 0, -i, i, 0, 1 if i < 0 else 2)
+            push(a, 1, 1, i, 0)
+            push(a, 1, -1, i, 0)
+        elif j in (1, -1):
+            push(a, 1, -j, i, j, 1 if j < 0 else 2)
         ref = block(a, i, j)
         k = slot(i, j)
         cp = remote(ref, ref, c_s.at[a, k], c_r.at[a, k], core)
@@ -143,61 +161,123 @@
     for a in (0, 1):
         for way in (1, -1):
             push(a, 0, way, 0, 0)
-    for a in (0, 1):
-        for way in (1, -1):
             push(a, 1, way, 0, 0)
-    for a in (0, 1):
-        for way in (1, -1):
-            arrived(a, -way, 0)
-            push(a, 0, way, -way, 0, 1 if way > 0 else 2)
-            push(a, 1, 1, -way, 0)
-            push(a, 1, -1, -way, 0)
-            share(a, -way, 0)
-    for i in OFFS:
-        for a in (0, 1):
-            if i == 2:
-                arrived(a, 2, 0)
-                push(a, 1, 1, 2, 0)
-                push(a, 1, -1, 2, 0)
-                share(a, 2, 0)
-        for a in (0, 1):
-            for way in (1, -1):
-                arrived(a, i, -way)
-                push(a, 1, way, i, -way, 1 if way > 0 else 2)
-                share(a, i, -way)
-    for i in OFFS:
-        for a in (0, 1):
-            arrived(a, i, 2)
-            share(a, i, 2)
-
-    theirs = pl.ds(pl.multiple_of((1 - c) * HALF, 128), HALF)
-    for a in (0, 1):
-        for i in OFFS:
-            for j in OFFS:
-                if (i, j) != (0, 0):
-                    if a == 0:
-                        zz, xx = (z + j + 4) % 4, (x + i + 4) % 4
-                    else:
-                        zz, xx = (z + i + 4) % 4, (x + j + 4) % 4
-                    ref = outs[a].at[
-                        pl.ds(pl.multiple_of((zz * 4 + xx) * ROWS, 16), ROWS), theirs
-                    ]
-                    k = slot(i, j)
-                    remote(ref, ref, c_s.at[a, k], c_r.at[a, k], core).wait_recv()
+
+    stored = []
+    tally = [0]
+
+    def store(src, dst):
+        cp = pltpu.make_async_copy(src, dst, out_sem.at[tally[0]])
+        tally[0] += 1
+        cp.start()
+        stored.append(cp)
+
+    def chunk_rows(k):
+        return pl.ds(pl.multiple_of(((z // 2 + k) % 2) * GROUP, 16), GROUP)
+
+    def chunk_ready(k):
+        for dz in ((0, 1), (-1, 2))[k]:
+            for a in (0, 1):
+                for dx in OFFS:
+                    i, j = (dx, dz) if a == 0 else (dz, dx)
+                    if (i, j) != (0, 0):
+                        ref = outs[a].at[place(a, i, j), theirs]
+                        at = slot(i, j)
+                        remote(ref, ref, c_s.at[a, at], c_r.at[a, at], core).wait_recv()
+        rows = chunk_rows(k)
+        store(n_ref.at[rows, :], n_hbm.at[rows, :])
+        store(g_ref.at[rows, :], g_hbm.at[rows, :])
+
+    def piece(k, f, w):
+        rows = chunk_rows(k)
+        normed = n_ref[rows, :]
+        gate = contract_cols(normed, wg[f:f + w, :])
+        up = contract_cols(normed, wu[f:f + w, :])
+        d_hidden = contract_cols(g_ref[rows, :], wd[f:f + w, :])
+        sigma = jax.nn.sigmoid(gate)
+        silu = gate * sigma
+        hidden = (silu * up).astype(BF)
+        d_gate = (d_hidden * up * sigma * (1.0 + gate * (1.0 - sigma))).astype(BF)
+        d_up = (d_hidden * silu).astype(BF)
+        if k == 0:
+            dg_ref[:, f:f + w] = d_gate
+            du_ref[:, f:f + w] = d_up
+        m = min(w, MAIN - f)
+        for q, value in enumerate((d_gate, d_up, hidden)):
+            x_ref[rows, q * MAIN + f:q * MAIN + f + m] = value[:, :m]
+        if m < w:
+            gap = jnp.zeros((GROUP, 32 - REM), BF)
+            x_ref[rows, 3 * MAIN:] = jnp.concatenate(
+                [d_gate[:, m:], gap, d_up[:, m:], gap, hidden[:, m:], gap,
+                 jnp.zeros((GROUP, 32), BF)],
+                axis=1,
+            )
+            store(x_ref.at[rows, :], x_hbm.at[rows, :])
+
+    def moves(*items):
+        for item in items:
+            arrive(*item)
+
+    moves((0, -1, 0), (1, 0, -1), (0, 1, 0), (1, 0, 1))
+    moves((1, 1, 0), (0, 0, 1), (0, 2, 0), (1, 0, 2))
+    moves((1, -1, 0), (0, 0, -1))
+    moves((0, -1, 1), (1, 1, -1), (0, 1, 1), (1, 1, 1))
+    moves((0, -1, -1), (1, -1, -1), (0, 1, -1), (1, -1, 1))
+    moves((0, 2, 1), (1, 1, 2))
+    for cp in weights:
+        cp.wait()
+    chunk_ready(0)
+    piece(0, *PIECES[0])
+    moves((1, 2, 0), (0, 0, 2), (1, -1, 2), (0, 2, -1))
+    piece(0, *PIECES[1])
+    moves((0, -1, 2), (0, 1, 2), (1, 2, -1), (1, 2, 1))
+    piece(0, *PIECES[2])
+    moves((0, 2, 2), (1, 2, 2))
+    piece(0, *PIECES[3])
+    chunk_ready(1)
+    for f, w in PIECES:
+        piece(1, f, w)
+
+    for k in range(8):
+        cols = slice(k * 512, (k + 1) * 512)
+        value = jnp.dot(dg_ref[...], wg[:, cols], preferred_element_type=F32)
+        value = value + jnp.dot(du_ref[...], wu[:, cols], preferred_element_type=F32)
+        p_ref[:, cols] = value.astype(BF)
+    store(p_ref, p_hbm)
     for cp in swaps + sent:
         cp.wait_send()
-
-
-def gather(layer_input, grad_out, gain):
+    for cp in stored:
+        cp.wait()
+
+
+def gather(layer_input, grad_out, gain, w_gate, w_up, w_down):
     vmem = pl.BlockSpec(memory_space=pltpu.VMEM)
+    hbm = pl.BlockSpec(memory_space=pl.ANY)
     dma = pltpu.SemaphoreType.DMA
+    v = pltpu.VMEM
     return pl.pallas_call(
         gather_kernel,
-        out_shape=[jax.ShapeDtypeStruct((PLANE, D), BF)] * 2,
-        in_specs=[vmem] * 3,
-        out_specs=[vmem] * 2,
+        out_shape=[
+            jax.ShapeDtypeStruct((PLANE, D), BF),
+            jax.ShapeDtypeStruct((PLANE, D), BF),
+            jax.ShapeDtypeStruct((PLANE, XW), BF),
+            jax.ShapeDtypeStruct((GROUP, D), BF),
+        ],
+        in_specs=[vmem] * 3 + [hbm] * 3,
+        out_specs=[hbm] * 4,
         scratch_shapes=[
-            pltpu.VMEM((2, 24, D), BF),
+            v((PLANE, D), BF),
+            v((PLANE, D), BF),
+            v((PLANE, XW), BF),
+            v((GROUP, CORE_FF), BF),
+            v((GROUP, CORE_FF), BF),
+            v((GROUP, D), BF),
+            v((CORE_FF, D), BF),
+            v((CORE_FF, D), BF),
+            v((CORE_FF, D), BF),
+            v((2, 24, D), BF),
+            dma((3,)),
+            dma((7,)),
             dma((2,)),
             dma((2,)),
             dma((2, 20)),
@@ -206,20 +286,20 @@
             dma((2, 16)),
         ],
         compiler_params=pltpu.CompilerParams(
-            collective_id=0, has_side_effects=True, vmem_limit_bytes=48 << 20
+            collective_id=0, has_side_effects=True, vmem_limit_bytes=60 << 20
         ),
-    )(layer_input, grad_out, gain)
-
-
-PART_A = (("n", 0, 512), ("n", 512, 512), ("h", 0, 400))
-PART_B = (("n", 1024, 512), ("n", 1536, 384), ("h", 400, 528))
+    )(layer_input, grad_out, gain, w_gate, w_up, w_down)
+
+
+PART_A = ((0, 512), (512, 512), (1792, 384))
+PART_B = ((1024, 384), (1408, 384), (2176, 608))
 NC = len(PART_A)
 
 
 def reduce_kernel(
     n_hbm, g_hbm, x_ref, p_ref, li_ref, gain_ref,
-    tn_out, th_out, ig_out, gain_out,
-    nb, gb, nt, ht, far_n, far_h, mid_n, mid_h, to_n, to_h, in_n, in_h, own_n, own_h,
+    t_out, ig_out, gain_out,
+    nb, gb, xt, far, mid, outgo, into, own,
     pc, q, xo, xi, xs, xr, zs, zr, dn, gs, gr,
     load, far_s, far_r, near_s, near_r, p_s, p_r, g_sem, g_rec,
 ):
@@ -254,43 +334,42 @@
     theirs = pl.ds(pl.multiple_of((1 - c) * HALF, 128), HALF)
     swap = send(p_ref.at[:, theirs], pc, p_s.at[0], p_r.at[0], core)
 
-    ht[0:MAIN, :] = x_ref[:, NW:XW].T
-    ht[MAIN:, :] = x_ref[:, NW - 128:NW].T
+    xt[...] = x_ref[...].T
 
     def ready(r):
         for cp in loads[r]:
             cp.wait()
-        nt[r % 4] = nb[r % 4].T
-
-    def term(r, chunk):
-        kind, s, w = chunk
-        if kind == "n":
-            return jnp.dot(nt[r % 4], x_ref[:, s:s + w], preferred_element_type=F32)
-        return jnp.dot(ht[s:s + w, :], gb[r % 4], preferred_element_type=F32)
-
-    def view(n, h, chunk):
-        kind, s, w = chunk
-        return n.at[:, pl.ds(s, w)] if kind == "n" else h.at[pl.ds(s, w), :]
+
+    def fill(ref, r, chunk, add=None):
+        k = r % 4
+        start, size = chunk
+        stop = start + size
+        marks = [m for m in (start, 2 * MAIN, 3 * MAIN, 3 * MAIN + 64, stop) if start <= m <= stop]
+        for p, e in zip(marks, marks[1:]):
+            if p == e:
+                continue
+            tokens = gb if 2 * MAIN <= p < 3 * MAIN or p >= 3 * MAIN + 64 else nb
+            value = jnp.dot(xt[p:e, :], tokens[k], preferred_element_type=F32)
+            if add is not None:
+                value = value + add[p:e, :].astype(F32)
+            ref[p:e, :] = value.astype(ref.dtype)
+
+    def view(ref, chunk):
+        return ref.at[pl.ds(*chunk), :]
 
     ready(2)
     for k in range(NC):
         for part, chunk in enumerate((PART_A[k], PART_B[k])):
-            ref = view(far_n, far_h, chunk)
-            ref[...] = term(2, chunk).astype(BF)
+            fill(far, 2, chunk)
             send(
-                ref, view(mid_n, mid_h, chunk), far_s.at[part, k], far_r.at[part, k],
+                view(far, chunk), view(mid, chunk), far_s.at[part, k], far_r.at[part, k],
                 ys_dev[part],
             )
 
     def near(part, chunk, k, which, extra):
-        r = 1 if part == 0 else -1
-        value = term(r, chunk)
-        if extra:
-            value = value + view(mid_n, mid_h, chunk)[...].astype(F32)
-        ref = view(to_n.at[part], to_h.at[part], chunk)
-        ref[...] = value.astype(BF)
+        fill(outgo.at[part], 1 if part == 0 else -1, chunk, mid if extra else None)
         send(
-            ref, view(in_n.at[part], in_h.at[part], chunk),
+            view(outgo.at[part], chunk), view(into.at[part], chunk),
             near_s.at[part, which, k], near_r.at[part, which, k], ys_dev[part],
         )
 
@@ -302,7 +381,7 @@
     ready(0)
     for k in range(NC):
         for chunk in (PART_A[k], PART_B[k]):
-            view(own_n, own_h, chunk)[...] = term(0, chunk)
+            fill(own, 0, chunk)
 
     swap.wait_recv()
     q[...] = p_ref[:, mine].astype(F32) + pc[...].astype(F32)
@@ -369,21 +448,21 @@
 
     for k in range(NC):
         for part, chunk in enumerate((PART_A[k], PART_B[k])):
-            ref = view(mid_n, mid_h, chunk)
+            ref = view(mid, chunk)
             remote(ref, ref, far_s.at[part, k], far_r.at[part, k], core).wait_recv()
             near(part, chunk, k, part, True)
 
     for which, parts in ((0, PART_A), (1, PART_B)):
         for k in range(NC):
             chunk = parts[k]
-            value = view(own_n, own_h, chunk)[...]
+            value = view(own, chunk)[...]
             for part in (0, 1):
-                ref = view(in_n.at[part], in_h.at[part], chunk)
+                ref = view(into.at[part], chunk)
                 remote(
                     ref, ref, near_s.at[part, which, k], near_r.at[part, which, k], core
                 ).wait_recv()
                 value = value + ref[...].astype(F32)
-            view(tn_out, th_out, chunk)[...] = value.astype(BF)
+            view(t_out, chunk)[...] = value.astype(BF)
     for cp in sent:
         cp.wait_send()
 
@@ -396,28 +475,21 @@
     return pl.pallas_call(
         reduce_kernel,
         out_shape=[
-            jax.ShapeDtypeStruct((BLK, NW), BF),
-            jax.ShapeDtypeStruct((HW, BLK), BF),
+            jax.ShapeDtypeStruct((TR, BLK), BF),
             jax.ShapeDtypeStruct((24, D), BF),
             jax.ShapeDtypeStruct((1, D), F32),
         ],
         in_specs=[hbm, hbm, vmem, vmem, vmem, vmem],
-        out_specs=[vmem] * 4,
+        out_specs=[vmem] * 3,
         scratch_shapes=[
             v((4, PLANE, BLK), BF),
             v((4, PLANE, BLK), BF),
-            v((4, BLK, PLANE), BF),
-            v((MAIN + 128, PLANE), BF),
-            v((BLK, NW), BF),
-            v((HW, BLK), BF),
-            v((BLK, NW), BF),
-            v((HW, BLK), BF),
-            v((2, BLK, NW), BF),
-            v((2, HW, BLK), BF),
-            v((2, BLK, NW), BF),
-            v((2, HW, BLK), BF),
-            v((BLK, NW), F32),
-            v((HW, BLK), F32),
+            v((XW, PLANE), BF),
+            v((TR, BLK), BF),
+            v((TR, BLK), BF),
+            v((2, TR, BLK), BF),
+            v((2, TR, BLK), BF),
+            v((TR, BLK), F32),
             v((GROUP, HALF), BF),
             v((GROUP, HALF), F32),
             v((2 * ROWS, HALF), BF),
@@ -445,48 +517,20 @@
     )(n, g, xp, p, layer_input, gain)
 
 
-def contract_cols(left, right):
-    return lax.dot_general(left, right, (((1,), (1,)), ((), ())), preferred_element_type=F32)
-
-
 def body(layer_input, gain_vector, w_gate, w_up, w_down, grad_out):
     gain = gain_vector[None, :]
-    normed, upstream = gather(layer_input, grad_out, gain)
-    gate = jnp.dot(normed, w_gate, preferred_element_type=F32)
-    up = jnp.dot(normed, w_up, preferred_element_type=F32)
-    sigma = jax.nn.sigmoid(gate)
-    silu = gate * sigma
-    hidden = (silu * up).astype(BF)
-    d_hidden = contract_cols(upstream, w_down)
-    d_gate = (d_hidden * up * sigma * (1.0 + gate * (1.0 - sigma))).astype(BF)
-    d_up = (d_hidden * silu).astype(BF)
-    start = (lax.axis_index("dp") % 2) * GROUP
-    own_gate = lax.dynamic_slice_in_dim(d_gate, start, GROUP, 0)
-    own_up = lax.dynamic_slice_in_dim(d_up, start, GROUP, 0)
-    share = (contract_cols(own_gate, w_gate) + contract_cols(own_up, w_up)).astype(BF)
-    packed = jnp.concatenate(
-        [
-            d_gate[:, :MAIN],
-            d_up[:, :MAIN],
-            hidden[:, MAIN:],
-            d_gate[:, MAIN:],
-            d_up[:, MAIN:],
-            jnp.zeros((PLANE, 128 - 3 * REM), BF),
-            hidden[:, :MAIN],
-        ],
-        axis=1,
+    normed, upstream, packed, share = gather(
+        layer_input, grad_out, gain, w_gate.T, w_up.T, w_down
     )
-    tn, th, input_gradient, gain_gradient = reduce(
+    terms, input_gradient, gain_gradient = reduce(
         normed, upstream, packed, share, layer_input, gain
     )
-    rest = 2 * MAIN + REM
-    return (
-        input_gradient,
-        gain_gradient[0],
-        jnp.concatenate([tn[:, :MAIN], tn[:, rest:rest + REM]], axis=1),
-        jnp.concatenate([tn[:, MAIN:2 * MAIN], tn[:, rest + REM:rest + 2 * REM]], axis=1),
-        th[:CORE_FF],
-    )
+
+    def unpack(k):
+        rest = 3 * MAIN + 32 * k
+        return jnp.concatenate([terms[k * MAIN:(k + 1) * MAIN], terms[rest:rest + REM]], axis=0)
+
+    return input_gradient, gain_gradient[0], unpack(0).T, unpack(1).T, unpack(2)
 
 
 def solution(mesh):

time: 224 us -> 191 us (0.85)
  matrix products: 41.2 us -> 0 us
  Pallas kernels: 161 us -> 184 us
  local copies, waits for them, and re-layouts: 19.7 us -> 4 us
    dot_general x5 -> x0, matrix products: 41.2 us -> none  [the longest x3 19.1 us: contract_cols(): lax.dot_general(left, right, (((1,), (1,)), ((), ())), preferred_element_...]
    pallas_call x1, Pallas kernels: 49.9 us -> 75.2 us  [gather(): pl.pallas_call(gather_kernel, out_shape=[jax.ShapeDtypeStruct((PLANE, D),...]
    concatenate x1 -> x0, local copies, waits for them, and re-layouts: 7.9 us -> none  [body(): jnp.concatenate([d_gate[:, :MAIN], d_up[:, :MAIN], hidden[:, MAIN:], d_ga...]
    unnamed x27 -> x6, local copies, waits for them, and re-layouts: 7.39 us -> 1.29 us
    pallas_call x1, Pallas kernels: 111 us -> 109 us  [reduce(): pl.pallas_call(reduce_kernel, out_shape=[jax.ShapeDtypeStruct((TR, BLK),...]
where the time goes in v2:
time: 191 us
  Pallas kernels  184 us (96%)
  local copies, waits for them, and re-layouts  4 us (2%)
  other arithmetic  2.37 us (1%)
    pallas_call x1, Pallas kernels, reduce(): pl.pallas_call(reduce_kernel, out_shape=[jax.ShapeDtypeStruct((TR, BLK),...  109 us
    pallas_call x1, Pallas kernels, gather(): pl.pallas_call(gather_kernel, out_shape=[jax.ShapeDtypeStruct((PLANE, D),...  75.2 us

profile of v2, /device:TPU:0, one launch (start us, length us, event | category | flops | bytes accessed | tf_op | source)
XLA Modules:
  0.0 191.1 jit_solution(4282200040929303552)
XLA Ops:
  0.6 75.2 %shard_map.101 = (bf16[768,4096]{1,0:T(8,128)(2,1)}, bf16[768,4096]{1,0:T(8,128)(2,1)}, bf16[768,2816]{1,0:T(8,128)(2,1)}, bf16[384,4096]{1,0:T(8,128)(2,1)}) custom-call(bf16[24,4096]{1,0:T(8,128)(2,1)} %li_ref.3, bf16[24,4096]{1,0:T(8,128)(2,1)} %go_ref.1, f32[1,4096]{1,0:T(1,128)} %bitcast.10, bf16[924,4096]{1,0:T(8,128)(2,1)} %bitcast.8, ...), custom_call_target="tpu_custom_call" | custom-call | tf_op jit(solution)/shard_map/pallas_call | solution.py:258
  75.9 108.9 %shard_map.102 = (bf16[2784,512]{1,0:T(8,128)(2,1)}, bf16[24,4096]{1,0:T(8,128)(2,1)}, f32[1,4096]{1,0:T(1,128)}) custom-call(bf16[768,4096]{1,0:T(8,128)(2,1)} %get-tuple-element.12.n_hbm, bf16[768,4096]{1,0:T(8,128)(2,1)} %get-tuple-element.13.g_hbm, bf16[768,2816]{1,0:T(8,128)(2,1)} %get-tuple-element.14.x_ref, ...), custom_call_target="tpu_custom_call" | custom-call | tf_op jit(solution)/shard_map/pallas_call | solution.py:475
  184.7 0.8 fusion.1
  185.5 1.9 fusion
  187.5 0.0 copy-start
  187.5 0.0 copy-start.1
  187.5 1.0 pad_maximum_fusion
  188.5 1.4 maximum_bitcast_fusion
  189.9 0.0 copy-done
  189.9 0.7 copy.13
  190.5 0.0 copy-done.1
  190.5 0.6 copy.14
Async XLA Ops:
  187.5 2.4 %copy-start = (bf16[24,4096]{1,0:T(8,128)(2,1)S(1)}, bf16[24,4096]{1,0:T(8,128)(2,1)}, u32[]{:S(2)}) copy-start(bf16[24,4096]{1,0:T(8,128)(2,1)} %get-tuple-element.32) | copy-start | bytes 589828
  187.5 3.1 %copy-start.1 = (f32[1,4096]{1,0:T(1,128)S(1)}, f32[1,4096]{1,0:T(1,128)}, u32[]{:S(2)}) copy-start(f32[1,4096]{1,0:T(1,128)} %get-tuple-element.17) | copy-start | bytes 49156

commit v3 on v2

--- a/solution.py
+++ b/solution.py
@@ -18,10 +18,12 @@
 GROUP = 384
 BLK = 512
 CORE_FF = 924
-MAIN = 896
-REM = CORE_FF - MAIN
-XW = 3 * MAIN + 128
-TR = 3 * MAIN + 96
+PIECES = ((0, 256, 0), (256, 208, 768), (464, 256, 1392), (720, 204, 2160))
+TR = 2784
+
+
+def padded(units):
+    return (units + 15) // 16 * 16
 
 
 def coords():
@@ -51,7 +53,6 @@
 
 
 OFFS = (0, -1, 1, 2)
-PIECES = ((0, 256), (256, 256), (512, 256), (768, 156))
 
 
 def slot(i, j):
@@ -63,22 +64,27 @@
 
 
 def gather_kernel(
-    li_ref, go_ref, gain_ref, wg_hbm, wu_hbm, wd_hbm, n_hbm, g_hbm, x_hbm, p_hbm,
-    n_ref, g_ref, x_ref, dg_ref, du_ref, p_ref, wg, wu, wd, other,
-    w_sem, out_sem, ex_s, ex_r, s_sem, r_sem, c_s, c_r,
+    li_ref, go_ref, gain_ref, wg_hbm, wu_hbm, wd_hbm,
+    n_hbm, g_hbm, xt_hbm, r_hbm, e_hbm, p_hbm,
+    ng, xt, dg_ref, du_ref, p_ref, wg, wu, wd, other, stage,
+    w_sem, out_sem, ex_s, ex_r, s_sem, r_sem, c_s, c_r, y_s, y_r, e_s, e_r,
 ):
     x, y, z, c = coords()
     s = 1 - 2 * (z % 2)
+    sy = 1 - 2 * (y % 2)
+    zh = z // 2
     core = device(x, y, z, 1 - c)
     step = {
         "x": (device(x + 1, y, z, c), device(x - 1, y, z, c)),
         "z": (device(x, y, z + s, c), device(x, y, z - s, c)),
     }
+    far = {"x": device(x + 2, y, z, c), "z": device(x, y, z + 2, c)}
+    near_y = (device(x, y + sy, z, c), device(x, y - sy, z, c))
     weights = [
         pltpu.make_async_copy(src, dst, w_sem.at[k])
         for k, (src, dst) in enumerate(((wg_hbm, wg), (wu_hbm, wu), (wd_hbm, wd)))
     ]
-    greet([core, *step["x"], *step["z"]])
+    greet([core, *step["x"], *step["z"], far["x"], far["z"], *near_y])
     swaps = []
     for a, ref in enumerate((li_ref, go_ref)):
         cp = remote(ref, other.at[a], ex_s.at[a], ex_r.at[a], core)
@@ -89,6 +95,7 @@
 
     base = pl.multiple_of((z * 4 + x) * ROWS, 16)
     first = c == 0
+    n_ref, g_ref = ng.at[0], ng.at[1]
     outs = (n_ref, g_ref)
 
     swaps[0].wait_recv()
@@ -163,6 +170,19 @@
             push(a, 0, way, 0, 0)
             push(a, 1, way, 0, 0)
 
+    def hop(src, dst, k, to):
+        cp = remote(src, dst, e_s.at[k], e_r.at[k], to)
+        cp.start()
+        sent.append(cp)
+
+    def landed(ref, k):
+        remote(ref, ref, e_s.at[k], e_r.at[k], core).wait_recv()
+
+    for q, to in enumerate(near_y):
+        for k, yy in enumerate((y + (sy if q == 0 else -sy), y + 2)):
+            cols = pl.ds(pl.multiple_of(((yy + 4) % 4) * 2 * BLK, 128), 2 * BLK)
+            hop(ng.at[c, pl.ds(base, ROWS), cols], stage.at[2 * q + k], 2 * q + k, to)
+
     stored = []
     tally = [0]
 
@@ -170,10 +190,41 @@
         cp = pltpu.make_async_copy(src, dst, out_sem.at[tally[0]])
         tally[0] += 1
         cp.start()
-        stored.append(cp)
+        return cp
+
+    def set_cols(which):
+        return pl.ds(pl.multiple_of(which * BLK, 128), BLK)
+
+    def extra_z():
+        for k in range(4):
+            landed(stage.at[k], k)
+        mine = e_hbm.at[c, :, z, x]
+        local = store(stage.at[:, :, set_cols(zh)], mine)
+        hop(stage.at[:, :, set_cols(zh)], mine, 4, step["z"][0])
+        hop(stage.at[:, :, set_cols(1 - zh)], mine, 5, step["z"][1])
+        hop(stage.at[:, :, set_cols(1 - zh)], mine, 6, far["z"])
+        return local
+
+    def extra_x(local):
+        local.wait()
+        for k, dz in ((4, 1), (5, -1), (6, 2)):
+            landed(e_hbm.at[c, :, (z + s * dz + 4) % 4, x], k)
+        mine = e_hbm.at[c, :, :, x]
+        hop(mine, mine, 7, step["x"][0])
+        hop(mine, mine, 8, step["x"][1])
+        hop(mine, mine, 9, far["x"])
+        hop(mine, mine, 10, core)
+
+    def extra_share(k, dx):
+        ref = e_hbm.at[c, :, :, (x + dx + 4) % 4]
+        landed(ref, k)
+        hop(ref, ref, k + 4, core)
+
+    def group_of(k):
+        return (zh + k) % 2
 
     def chunk_rows(k):
-        return pl.ds(pl.multiple_of(((z // 2 + k) % 2) * GROUP, 16), GROUP)
+        return pl.ds(pl.multiple_of(group_of(k) * GROUP, 16), GROUP)
 
     def chunk_ready(k):
         for dz in ((0, 1), (-1, 2))[k]:
@@ -185,10 +236,16 @@
                         at = slot(i, j)
                         remote(ref, ref, c_s.at[a, at], c_r.at[a, at], core).wait_recv()
         rows = chunk_rows(k)
-        store(n_ref.at[rows, :], n_hbm.at[rows, :])
-        store(g_ref.at[rows, :], g_hbm.at[rows, :])
-
-    def piece(k, f, w):
+        stored.append(store(n_ref.at[rows, :], n_hbm.at[rows, :]))
+        stored.append(store(g_ref.at[rows, :], g_hbm.at[rows, :]))
+
+    def term_view(ref, k, p):
+        _, w, row = PIECES[p]
+        lanes = pl.ds(pl.multiple_of(group_of(k) * GROUP, 128), GROUP)
+        return ref.at[pl.ds(row, 3 * padded(w)), lanes]
+
+    def piece(k, p):
+        f, w, row = PIECES[p]
         rows = chunk_rows(k)
         normed = n_ref[rows, :]
         gate = contract_cols(normed, wg[f:f + w, :])
@@ -196,23 +253,25 @@
         d_hidden = contract_cols(g_ref[rows, :], wd[f:f + w, :])
         sigma = jax.nn.sigmoid(gate)
         silu = gate * sigma
-        hidden = (silu * up).astype(BF)
-        d_gate = (d_hidden * up * sigma * (1.0 + gate * (1.0 - sigma))).astype(BF)
-        d_up = (d_hidden * silu).astype(BF)
+        hidden = silu * up
+        d_gate = d_hidden * up * sigma * (1.0 + gate * (1.0 - sigma))
+        d_up = d_hidden * silu
         if k == 0:
-            dg_ref[:, f:f + w] = d_gate
-            du_ref[:, f:f + w] = d_up
-        m = min(w, MAIN - f)
+            dg_ref[:, f:f + w] = d_gate.astype(BF)
+            du_ref[:, f:f + w] = d_up.astype(BF)
+        size = padded(w)
+        lanes = pl.ds(pl.multiple_of(group_of(k) * GROUP, 128), GROUP)
         for q, value in enumerate((d_gate, d_up, hidden)):
-            x_ref[rows, q * MAIN + f:q * MAIN + f + m] = value[:, :m]
-        if m < w:
-            gap = jnp.zeros((GROUP, 32 - REM), BF)
-            x_ref[rows, 3 * MAIN:] = jnp.concatenate(
-                [d_gate[:, m:], gap, d_up[:, m:], gap, hidden[:, m:], gap,
-                 jnp.zeros((GROUP, 32), BF)],
-                axis=1,
-            )
-            store(x_ref.at[rows, :], x_hbm.at[rows, :])
+            if w < 256:
+                value = jnp.concatenate([value, jnp.zeros((GROUP, 256 - w), F32)], axis=1)
+            xt[row + q * size:row + (q + 1) * size, lanes] = value.T[:size].astype(BF)
+        cp = remote(
+            term_view(xt, k, p), term_view(r_hbm, k, p),
+            y_s.at[k, p], y_r.at[k, p], near_y[p // 2],
+        )
+        cp.start()
+        sent.append(cp)
+        stored.append(store(term_view(xt, k, p), term_view(xt_hbm, k, p)))
 
     def moves(*items):
         for item in items:
@@ -227,23 +286,41 @@
     for cp in weights:
         cp.wait()
     chunk_ready(0)
-    piece(0, *PIECES[0])
+    piece(0, 0)
     moves((1, 2, 0), (0, 0, 2), (1, -1, 2), (0, 2, -1))
-    piece(0, *PIECES[1])
+    piece(0, 2)
     moves((0, -1, 2), (0, 1, 2), (1, 2, -1), (1, 2, 1))
-    piece(0, *PIECES[2])
+    piece(0, 1)
     moves((0, 2, 2), (1, 2, 2))
-    piece(0, *PIECES[3])
+    local = extra_z()
+    piece(0, 3)
     chunk_ready(1)
-    for f, w in PIECES:
-        piece(1, f, w)
-
-    for k in range(8):
+    piece(1, 0)
+    extra_x(local)
+    piece(1, 2)
+    piece(1, 1)
+    piece(1, 3)
+
+    def share(k):
         cols = slice(k * 512, (k + 1) * 512)
         value = jnp.dot(dg_ref[...], wg[:, cols], preferred_element_type=F32)
         value = value + jnp.dot(du_ref[...], wu[:, cols], preferred_element_type=F32)
         p_ref[:, cols] = value.astype(BF)
-    store(p_ref, p_hbm)
+
+    for k in range(4):
+        share(k)
+    extra_share(7, -1)
+    extra_share(8, 1)
+    for k in range(4, 8):
+        share(k)
+    stored.append(store(p_ref, p_hbm))
+    extra_share(9, 2)
+    for k, dx in ((10, 0), (11, -1), (12, 1), (13, 2)):
+        landed(e_hbm.at[1 - c, :, :, (x + dx + 4) % 4], k)
+    for k in (0, 1):
+        for p in range(4):
+            ref = term_view(r_hbm, k, p)
+            remote(ref, ref, y_s.at[k, p], y_r.at[k, p], core).wait_recv()
     for cp in swaps + sent:
         cp.wait_send()
     for cp in stored:
@@ -260,15 +337,16 @@
         out_shape=[
             jax.ShapeDtypeStruct((PLANE, D), BF),
             jax.ShapeDtypeStruct((PLANE, D), BF),
-            jax.ShapeDtypeStruct((PLANE, XW), BF),
+            jax.ShapeDtypeStruct((TR, PLANE), BF),
+            jax.ShapeDtypeStruct((TR, PLANE), BF),
+            jax.ShapeDtypeStruct((2, 4, 4, 4, ROWS, BLK), BF),
             jax.ShapeDtypeStruct((GROUP, D), BF),
         ],
         in_specs=[vmem] * 3 + [hbm] * 3,
-        out_specs=[hbm] * 4,
+        out_specs=[hbm] * 6,
         scratch_shapes=[
-            v((PLANE, D), BF),
-            v((PLANE, D), BF),
-            v((PLANE, XW), BF),
+            v((2, PLANE, D), BF),
+            v((TR, PLANE), BF),
             v((GROUP, CORE_FF), BF),
             v((GROUP, CORE_FF), BF),
             v((GROUP, D), BF),
@@ -276,14 +354,19 @@
             v((CORE_FF, D), BF),
             v((CORE_FF, D), BF),
             v((2, 24, D), BF),
+            v((4, ROWS, 2 * BLK), BF),
             dma((3,)),
-            dma((7,)),
+            dma((14,)),
             dma((2,)),
             dma((2,)),
             dma((2, 20)),
             dma((2, 16, 2)),
             dma((2, 16)),
             dma((2, 16)),
+            dma((2, 4)),
+            dma((2, 4)),
+            dma((14,)),
+            dma((14,)),
         ],
         compiler_params=pltpu.CompilerParams(
             collective_id=0, has_side_effects=True, vmem_limit_bytes=60 << 20
@@ -291,36 +374,55 @@
     )(layer_input, grad_out, gain, w_gate, w_up, w_down)
 
 
-PART_A = ((0, 512), (512, 512), (1792, 384))
-PART_B = ((1024, 384), (1408, 384), (2176, 608))
-NC = len(PART_A)
-
-
 def reduce_kernel(
-    n_hbm, g_hbm, x_ref, p_ref, li_ref, gain_ref,
+    n_hbm, g_hbm, e_hbm, xt, rt, p_ref, li_ref, gain_ref,
     t_out, ig_out, gain_out,
-    nb, gb, xt, far, mid, outgo, into, own,
+    nb, eb, outgo, into, own,
     pc, q, xo, xi, xs, xr, zs, zr, dn, gs, gr,
-    load, far_s, far_r, near_s, near_r, p_s, p_r, g_sem, g_rec,
+    load, t_s, t_r, p_s, p_r, g_sem, g_rec,
 ):
     x, y, z, c = coords()
     zl, zh = z % 2, z // 2
+    sy = 1 - 2 * (y % 2)
     core = device(x, y, z, 1 - c)
     xs_dev = [device(x + k, y, z, c) for k in (1, -1, 2)]
     ys_dev = [device(x, y + k, z, c) for k in (1, -1, 2)]
     zs_dev = [device(x, y, z + k, c) for k in (1, -1, 2)]
     zpair = device(x, y, zh * 2 + 1 - zl, c)
+    alpha, beta = device(x, y + sy, z, c), device(x, y - sy, z, c)
 
     loads = {}
-    for r in (2, 1, -1, 0):
-        k = r % 4
-        cols = pl.ds(pl.multiple_of((((y + r + 4) % 4) * 2 + zh) * BLK, 128), BLK)
-        loads[r] = [
-            pltpu.make_async_copy(n_hbm.at[:, cols], nb.at[k], load.at[0, k]),
-            pltpu.make_async_copy(g_hbm.at[:, cols], gb.at[k], load.at[1, k]),
+
+    def fetch(b):
+        yy = (y + (0, sy, -sy)[b] + 4) % 4
+        cols = pl.ds(pl.multiple_of((yy * 2 + zh) * BLK, 128), BLK)
+        loads["n", b] = [
+            pltpu.make_async_copy(n_hbm.at[:, cols], nb.at[0, b], load.at[0, b]),
+            pltpu.make_async_copy(g_hbm.at[:, cols], nb.at[1, b], load.at[1, b]),
         ]
-        for cp in loads[r]:
+        for cp in loads["n", b]:
             cp.start()
+
+    def fetch_extra(b):
+        loads["e", b] = [
+            pltpu.make_async_copy(e_hbm.at[a, b], eb.at[a, b], load.at[a, 3 + b]) for a in (0, 1)
+        ]
+        for cp in loads["e", b]:
+            cp.start()
+
+    fetch(2)
+    fetch_extra(1)
+    fetch(1)
+    fetch_extra(3)
+    fetch(0)
+    fetch_extra(0)
+    fetch_extra(2)
+
+    def ready(*keys):
+        for key in keys:
+            for cp in loads[key]:
+                cp.wait()
+
     greet([core, *xs_dev, *ys_dev, *zs_dev])
     sent = []
 
@@ -334,54 +436,32 @@
     theirs = pl.ds(pl.multiple_of((1 - c) * HALF, 128), HALF)
     swap = send(p_ref.at[:, theirs], pc, p_s.at[0], p_r.at[0], core)
 
-    xt[...] = x_ref[...].T
-
-    def ready(r):
-        for cp in loads[r]:
-            cp.wait()
-
-    def fill(ref, r, chunk, add=None):
-        k = r % 4
-        start, size = chunk
-        stop = start + size
-        marks = [m for m in (start, 2 * MAIN, 3 * MAIN, 3 * MAIN + 64, stop) if start <= m <= stop]
-        for p, e in zip(marks, marks[1:]):
-            if p == e:
-                continue
-            tokens = gb if 2 * MAIN <= p < 3 * MAIN or p >= 3 * MAIN + 64 else nb
-            value = jnp.dot(xt[p:e, :], tokens[k], preferred_element_type=F32)
-            if add is not None:
-                value = value + add[p:e, :].astype(F32)
-            ref[p:e, :] = value.astype(ref.dtype)
-
-    def view(ref, chunk):
-        return ref.at[pl.ds(*chunk), :]
-
-    ready(2)
-    for k in range(NC):
-        for part, chunk in enumerate((PART_A[k], PART_B[k])):
-            fill(far, 2, chunk)
-            send(
-                view(far, chunk), view(mid, chunk), far_s.at[part, k], far_r.at[part, k],
-                ys_dev[part],
-            )
-
-    def near(part, chunk, k, which, extra):
-        fill(outgo.at[part], 1 if part == 0 else -1, chunk, mid if extra else None)
-        send(
-            view(outgo.at[part], chunk), view(into.at[part], chunk),
-            near_s.at[part, which, k], near_r.at[part, which, k], ys_dev[part],
-        )
-
-    ready(1)
-    ready(-1)
-    for k in range(NC):
-        near(0, PART_B[k], k, 1, False)
-        near(1, PART_A[k], k, 0, False)
-    ready(0)
-    for k in range(NC):
-        for chunk in (PART_A[k], PART_B[k]):
-            fill(own, 0, chunk)
+    def ranges(p):
+        _, w, row = PIECES[p]
+        w = padded(w)
+        return ((row, 2 * w, 0), (row + 2 * w, w, 1))
+
+    def term(rng, b, e):
+        row, size, a = rng
+        rows = slice(row, row + size)
+        value = jnp.dot(xt[rows, :], nb[a, b], preferred_element_type=F32)
+        return value + jnp.dot(rt[rows, :], eb[a, e], preferred_element_type=F32)
+
+    for k in (0, 1):
+        for half, (b, e, to) in enumerate(((2, 1, beta), (1, 3, alpha))):
+            if k == 0:
+                ready(("n", b), ("e", e))
+            p = 2 * half + k
+            for rng in ranges(p):
+                row, size, a = rng
+                outgo[row:row + size, :] = term(rng, b, e).astype(BF)
+                rows = pl.ds(row, size)
+                send(outgo.at[rows, :], into.at[rows, :], t_s.at[p, a], t_r.at[p, a], to)
+    ready(("n", 0), ("e", 0), ("e", 2))
+    for p in range(4):
+        for rng in ranges(p):
+            row, size, _ = rng
+            own[row:row + size, :] = term(rng, 0, 0 if p < 2 else 2)
 
     swap.wait_recv()
     q[...] = p_ref[:, mine].astype(F32) + pc[...].astype(F32)
@@ -446,28 +526,18 @@
             total = total + gr[s, k]
     gain_out[...] = total
 
-    for k in range(NC):
-        for part, chunk in enumerate((PART_A[k], PART_B[k])):
-            ref = view(mid, chunk)
-            remote(ref, ref, far_s.at[part, k], far_r.at[part, k], core).wait_recv()
-            near(part, chunk, k, part, True)
-
-    for which, parts in ((0, PART_A), (1, PART_B)):
-        for k in range(NC):
-            chunk = parts[k]
-            value = view(own, chunk)[...]
-            for part in (0, 1):
-                ref = view(into.at[part], chunk)
-                remote(
-                    ref, ref, near_s.at[part, which, k], near_r.at[part, which, k], core
-                ).wait_recv()
-                value = value + ref[...].astype(F32)
-            view(t_out, chunk)[...] = value.astype(BF)
+    for k in (0, 1):
+        for p in (k, k + 2):
+            for row, size, a in ranges(p):
+                rows = pl.ds(row, size)
+                ref = into.at[rows, :]
+                remote(ref, ref, t_s.at[p, a], t_r.at[p, a], core).wait_recv()
+                t_out[rows, :] = (own[rows, :] + ref[...].astype(F32)).astype(BF)
     for cp in sent:
         cp.wait_send()
 
 
-def reduce(n, g, xp, p, layer_input, gain):
+def reduce(n, g, e, xt, rt, p, layer_input, gain):
     vmem = pl.BlockSpec(memory_space=pltpu.VMEM)
     hbm = pl.BlockSpec(memory_space=pl.ANY)
     dma = pltpu.SemaphoreType.DMA
@@ -479,16 +549,13 @@
             jax.ShapeDtypeStruct((24, D), BF),
             jax.ShapeDtypeStruct((1, D), F32),
         ],
-        in_specs=[hbm, hbm, vmem, vmem, vmem, vmem],
+        in_specs=[hbm] * 3 + [vmem] * 5,
         out_specs=[vmem] * 3,
         scratch_shapes=[
-            v((4, PLANE, BLK), BF),
-            v((4, PLANE, BLK), BF),
-            v((XW, PLANE), BF),
+            v((2, 3, PLANE, BLK), BF),
+            v((2, 4, PLANE, BLK), BF),
             v((TR, BLK), BF),
             v((TR, BLK), BF),
-            v((2, TR, BLK), BF),
-            v((2, TR, BLK), BF),
             v((TR, BLK), F32),
             v((GROUP, HALF), BF),
             v((GROUP, HALF), F32),
@@ -501,11 +568,9 @@
             v((24, D), F32),
             v((4, 1, D), F32),
             v((4, 3, 1, D), F32),
-            dma((2, 4)),
-            dma((2, NC)),
-            dma((2, NC)),
-            dma((2, 2, NC)),
-            dma((2, 2, NC)),
+            dma((2, 7)),
+            dma((4, 2)),
+            dma((4, 2)),
             dma((7,)),
             dma((7,)),
             dma((4, 3)),
@@ -514,21 +579,25 @@
         compiler_params=pltpu.CompilerParams(
             collective_id=1, has_side_effects=True, vmem_limit_bytes=60 << 20
         ),
-    )(n, g, xp, p, layer_input, gain)
+    )(n, g, e, xt, rt, p, layer_input, gain)
 
 
 def body(layer_input, gain_vector, w_gate, w_up, w_down, grad_out):
     gain = gain_vector[None, :]
-    normed, upstream, packed, share = gather(
+    normed, upstream, terms_t, near_t, extra, share = gather(
         layer_input, grad_out, gain, w_gate.T, w_up.T, w_down
     )
     terms, input_gradient, gain_gradient = reduce(
-        normed, upstream, packed, share, layer_input, gain
+        normed, upstream, extra.reshape(2, 4, PLANE, BLK), terms_t, near_t, share,
+        layer_input, gain,
     )
 
     def unpack(k):
-        rest = 3 * MAIN + 32 * k
-        return jnp.concatenate([terms[k * MAIN:(k + 1) * MAIN], terms[rest:rest + REM]], axis=0)
+        parts = []
+        for _, w, row in PIECES:
+            first = row + k * padded(w)
+            parts.append(terms[first:first + w])
+        return jnp.concatenate(parts, axis=0)
 
     return input_gradient, gain_gradient[0], unpack(0).T, unpack(1).T, unpack(2)
 

time: 191 us -> 174 us (0.911)
  Pallas kernels: 184 us -> 166 us
    pallas_call x1, Pallas kernels: 109 us -> 57.9 us  [reduce(): pl.pallas_call(reduce_kernel, out_shape=[jax.ShapeDtypeStruct((TR, BLK),...]
    pallas_call x1, Pallas kernels: 75.2 us -> 108 us  [gather(): pl.pallas_call(gather_kernel, out_shape=[jax.ShapeDtypeStruct((PLANE, D),...]
where the time goes in v3:
time: 174 us
  Pallas kernels  166 us (95%)
  local copies, waits for them, and re-layouts  5.1 us (3%)
  other arithmetic  2.37 us (1%)
    pallas_call x1, Pallas kernels, gather(): pl.pallas_call(gather_kernel, out_shape=[jax.ShapeDtypeStruct((PLANE, D),...  108 us
    pallas_call x1, Pallas kernels, reduce(): pl.pallas_call(reduce_kernel, out_shape=[jax.ShapeDtypeStruct((TR, BLK),...  57.9 us
    slice x3, local copies, waits for them, and re-layouts, unpack(): parts.append(terms[first:first + w])  3.81 us

profile of v3, /device:TPU:0, one launch (start us, length us, event | category | flops | bytes accessed | tf_op | source)
XLA Modules:
  0.0 174.2 jit_solution(13069643991794160797)
XLA Ops:
  0.6 108.2 %shard_map.101 = (bf16[768,4096]{1,0:T(8,128)(2,1)}, bf16[768,4096]{1,0:T(8,128)(2,1)}, bf16[2784,768]{1,0:T(8,128)(2,1)}, bf16[2784,768]{1,0:T(8,128)(2,1)}, bf...) custom-call(bf16[24,4096]{1,0:T(8,128)(2,1)} %li_ref.3, bf16[24,4096]{1,0:T(8,128)(2,1)} %go_ref.1, ...), custom_call_target="tpu_custom_call" | custom-call | tf_op jit(solution)/shard_map/pallas_call | solution.py:335
  108.8 57.9 %shard_map.102 = (bf16[2784,512]{1,0:T(8,128)(2,1)}, bf16[24,4096]{1,0:T(8,128)(2,1)}, f32[1,4096]{1,0:T(1,128)}) custom-call(bf16[768,4096]{1,0:T(8,128)(2,1)} %get-tuple-element.14.n_hbm, bf16[768,4096]{1,0:T(8,128)(2,1)} %get-tuple-element.15.g_hbm, bf16[2,4,768,512]{3,2,1,0:T(8,128)(2,1)} %bitcast.11, bf16[2784,768]{1,0:T(8,128)(2,1)} %get-tuple-element.17.xt, ...), custom_call_target="tpu_custom_call" | custom-call | tf_op jit(solution)/shard_map/pallas_call | solution.py:545
  166.7 1.2 fusion.2
  167.9 1.2 fusion.1
  169.1 1.5 fusion
  170.5 1.0 pad_maximum_fusion
  171.5 0.0 copy-start
  171.5 0.0 copy-start.1
  171.5 1.4 maximum_bitcast_fusion
  172.9 0.0 copy-done
  172.9 0.7 copy.13
  173.6 0.0 copy-done.1
  173.6 0.6 copy.14
Async XLA Ops:
  171.5 1.4 copy-start
  171.5 2.1 %copy-start.1 = (f32[1,4096]{1,0:T(1,128)S(1)}, f32[1,4096]{1,0:T(1,128)}, u32[]{:S(2)}) copy-start(f32[1,4096]{1,0:T(1,128)} %get-tuple-element.21) | copy-start | bytes 49156
